TPU v7x, 32 devices: a whole 2x2x4 slice. The times are simulated.
32 devices in a mesh: dp: 8 (over z, x), tensor: 4 (over y, core).
Axes of the slice: x: 2, y: 2, z: 4, core: 2. Of those that a mesh axis runs over, the one named last changes fastest.
Arguments:
- tokens: bfloat16 [8, 2048, 1280], P('dp', 'tensor'), may hold values from -6 to 6
- segment_ids: int32 [8, 2048], P('dp'), may hold values from 0 to 2047, as said below
- adapter_choice: int32 [8], P('dp'), may hold values from 0 to 7, as said below
- cotangent: bfloat16 [8, 2048, 1280], P('dp', 'tensor'), may hold values from -6 to 6
- weight_query: bfloat16 [1280, 1280], P(None, 'tensor'), may hold values from -0.15625 to 0.15625
- weight_key: bfloat16 [1280, 1280], P(None, 'tensor'), may hold values from -0.15625 to 0.15625
- weight_value: bfloat16 [1280, 1280], P(None, 'tensor'), may hold values from -0.15625 to 0.15625
- weight_output: bfloat16 [1280, 1280], P(None, 'tensor'), may hold values from -0.625 to 0.625
- weight_upward: bfloat16 [1280, 1280], P(None, 'tensor'), may hold values from -0.15625 to 0.15625
- weight_downward: bfloat16 [1280, 1280], P(None, 'tensor'), may hold values from -0.15625 to 0.15625
- query_lower: bfloat16 [8, 16, 1280], replicated, may hold values from -0.15625 to 0.15625
- query_raise: bfloat16 [8, 16, 1280], P(None, None, 'tensor'), may hold values from -1.5 to 1.5
- key_lower: bfloat16 [8, 16, 1280], replicated, may hold values from -0.15625 to 0.15625
- key_raise: bfloat16 [8, 16, 1280], P(None, None, 'tensor'), may hold values from -1.5 to 1.5
- value_lower: bfloat16 [8, 16, 1280], replicated, may hold values from -0.15625 to 0.15625
- value_raise: bfloat16 [8, 16, 1280], P(None, None, 'tensor'), may hold values from -1.5 to 1.5
- output_lower: bfloat16 [8, 16, 1280], P(None, None, 'tensor'), may hold values from -0.625 to 0.625
- output_raise: bfloat16 [8, 16, 1280], replicated, may hold values from -1.5 to 1.5
- upward_lower: bfloat16 [8, 16, 1280], replicated, may hold values from -0.15625 to 0.15625
- upward_raise: bfloat16 [8, 16, 1280], P(None, None, 'tensor'), may hold values from -1.5 to 1.5
- downward_lower: bfloat16 [8, 16, 1280], P(None, None, 'tensor'), may hold values from -0.15625 to 0.15625
- downward_raise: bfloat16 [8, 16, 1280], replicated, may hold values from -1.5 to 1.5
Outputs:
- activations: bfloat16 [8, 2048, 1280], P('dp', 'tensor')
- input_grad: bfloat16 [8, 2048, 1280], P('dp', 'tensor')
- grad_query_lower: float32 [8, 16, 1280], replicated
- grad_query_raise: float32 [8, 16, 1280], P(None, None, 'tensor')
- grad_key_lower: float32 [8, 16, 1280], replicated
- grad_key_raise: float32 [8, 16, 1280], P(None, None, 'tensor')
- grad_value_lower: float32 [8, 16, 1280], replicated
- grad_value_raise: float32 [8, 16, 1280], P(None, None, 'tensor')
- grad_output_lower: float32 [8, 16, 1280], P(None, None, 'tensor')
- grad_output_raise: float32 [8, 16, 1280], replicated
- grad_upward_lower: float32 [8, 16, 1280], replicated
- grad_upward_raise: float32 [8, 16, 1280], P(None, None, 'tensor')
- grad_downward_lower: float32 [8, 16, 1280], P(None, None, 'tensor')
- grad_downward_raise: float32 [8, 16, 1280], replicated
Inputs may be any that keep to these rules, and one draw needn't show every extreme that they name: `segment_ids`: in each row the document numbers start at 0 and never fall, and may skip values; the last document of each row is numbered 2048 - 1; one document of each row begins before position 512 and covers position 1536. `adapter_choice`: set 0 and set 8 - 1 are each picked by some sequence; one set among 1 to 6 is picked by no sequence.
All inputs are finite; a program needn't handle non-finite values.
Results may differ from a plain program's by a relative error of at most 0.019.
Values may be sent and summed in bfloat16 or wider, within the bound.
A program may use at most 192 MiB of HBM per device.

v0:
```python
import jax
import jax.numpy as jnp
from jax import lax
from jax.sharding import PartitionSpec as P

HD = 80


EPS = 1e-06
NEG = -1e30
FULL_PRECISION = lax.Precision.HIGHEST


def rms_parts(values):
    factor = lax.rsqrt(jnp.mean(values * values, axis=-1, keepdims=True) + EPS)
    return (values * factor, factor)


def rms_back(grad, normed, factor):
    return factor * (grad - normed * jnp.mean(grad * normed, axis=-1, keepdims=True))


def dot_last(left, right):
    return lax.dot_general(
        left, right, (((1,), (1,)), ((), ())), preferred_element_type=jnp.float32
    )


def dot_first(left, right):
    return lax.dot_general(
        left, right, (((0,), (0,)), ((), ())), preferred_element_type=jnp.float32
    )


def dot_plain(left, right):
    return jnp.dot(left, right, preferred_element_type=jnp.float32)


def on_device(
    tokens,
    segment_ids,
    adapter_choice,
    cotangent,
    weight_query,
    weight_key,
    weight_value,
    weight_output,
    weight_upward,
    weight_downward,
    query_lower,
    query_raise,
    key_lower,
    key_raise,
    value_lower,
    value_raise,
    output_lower,
    output_raise,
    upward_lower,
    upward_raise,
    downward_lower,
    downward_raise,
):
    set_count = query_lower.shape[0]
    adapter_rank = query_lower.shape[1]
    chosen = (jnp.arange(set_count, dtype=jnp.int32) == adapter_choice[0]).astype(jnp.bfloat16)

    def pick_set(stacked):
        return jnp.einsum("s,srd->rd", chosen, stacked, preferred_element_type=jnp.float32).astype(
            jnp.bfloat16
        )

    chosen_query_lower = pick_set(query_lower)
    chosen_query_raise = pick_set(query_raise)
    chosen_key_lower = pick_set(key_lower)
    chosen_key_raise = pick_set(key_raise)
    chosen_value_lower = pick_set(value_lower)
    chosen_value_raise = pick_set(value_raise)
    chosen_output_lower = pick_set(output_lower)
    chosen_output_raise = pick_set(output_raise)
    chosen_upward_lower = pick_set(upward_lower)
    chosen_upward_raise = pick_set(upward_raise)
    chosen_downward_lower = pick_set(downward_lower)
    chosen_downward_raise = pick_set(downward_raise)
    resid_in = tokens[0].astype(jnp.float32)
    segments = segment_ids[0]
    length = segments.shape[0]
    local_width = weight_query.shape[1]
    local_heads = local_width // HD
    score_scale = HD ** (-0.5)
    block_rows = min(512, length)
    block_count = length // block_rows
    positions = jnp.arange(length, dtype=jnp.int32)
    unit_in, factor_in = rms_parts(resid_in)
    normed_in = unit_in.astype(jnp.bfloat16)
    normed_all = lax.all_gather(normed_in, "tensor", axis=0, tiled=True)
    lower_qkv = jnp.concatenate([chosen_query_lower, chosen_key_lower, chosen_value_lower], axis=0)
    low_qkv = dot_last(normed_all, lower_qkv).astype(jnp.bfloat16)
    low_query = low_qkv[:, :adapter_rank]
    low_key = low_qkv[:, adapter_rank : 2 * adapter_rank]
    low_value = low_qkv[:, 2 * adapter_rank :]

    def project(weight, low_part, raise_part):
        summed = dot_plain(normed_all, weight) + dot_plain(low_part, raise_part)
        return summed.astype(jnp.bfloat16).reshape(length, local_heads, HD)

    queries = project(weight_query, low_query, chosen_query_raise)
    keys_all = project(weight_key, low_key, chosen_key_raise)
    values_all = project(weight_value, low_value, chosen_value_raise)

    def masked_scores(query_piece, first_row):
        products = jnp.einsum(
            "qhd,khd->hqk", query_piece, keys_all, preferred_element_type=jnp.float32
        )
        query_positions = first_row + jnp.arange(block_rows, dtype=jnp.int32)
        query_segments = lax.dynamic_slice_in_dim(segments, first_row, block_rows)
        allowed = (query_segments[:, None] == segments[None, :]) & (
            positions[None, :] <= query_positions[:, None]
        )
        return jnp.where(allowed[None], products * score_scale, NEG)

    def forward_block(block_index):
        first_row = block_index * block_rows
        query_piece = lax.dynamic_slice_in_dim(queries, first_row, block_rows, 0)
        scores = masked_scores(query_piece, first_row)
        row_max = jnp.max(scores, axis=-1, keepdims=True)
        exponent = jnp.exp(scores - row_max)
        row_total = jnp.sum(exponent, axis=-1, keepdims=True)
        probabilities = (exponent / row_total).astype(jnp.bfloat16)
        block_out = jnp.einsum(
            "hqk,khd->qhd", probabilities, values_all, preferred_element_type=jnp.float32
        )
        return (block_out.astype(jnp.bfloat16), (row_max + jnp.log(row_total))[..., 0])

    attended_blocks, log_totals = lax.map(forward_block, jnp.arange(block_count, dtype=jnp.int32))
    attended = attended_blocks.reshape(length, local_width)
    low_out = dot_last(attended, chosen_output_lower)
    attn_terms = dot_last(attended, weight_output) + dot_plain(
        low_out, chosen_output_raise.astype(jnp.float32)
    )
    attn_local = lax.psum_scatter(attn_terms, "tensor", scatter_dimension=0, tiled=True)
    middle = resid_in + attn_local
    unit_mid, factor_mid = rms_parts(middle)
    normed_mid = unit_mid.astype(jnp.bfloat16)
    raise_down_wide = chosen_downward_raise.astype(jnp.float32)
    grad_out = cotangent[0]
    mid_all = lax.all_gather(normed_mid, "tensor", axis=0, tiled=True)
    low_upward = dot_last(mid_all, chosen_upward_lower).astype(jnp.bfloat16)
    preact = dot_plain(mid_all, weight_upward) + dot_plain(low_upward, chosen_upward_raise)
    activated = jax.nn.silu(preact).astype(jnp.bfloat16)
    low_downward = dot_last(activated, chosen_downward_lower)
    mlp_terms = dot_last(activated, weight_downward) + dot_plain(low_downward, raise_down_wide)
    mlp_local = lax.psum_scatter(
        mlp_terms.astype(jnp.bfloat16), "tensor", scatter_dimension=0, tiled=True
    ).astype(jnp.float32)
    activations = (middle + mlp_local).astype(jnp.bfloat16)
    grad_out_all = lax.all_gather(grad_out, "tensor", axis=0, tiled=True)
    grad_low_down = dot_last(grad_out_all, chosen_downward_raise).astype(jnp.bfloat16)
    grad_act = dot_plain(grad_out_all, weight_downward) + dot_plain(
        grad_low_down, chosen_downward_lower
    )
    sigma_pre = jax.nn.sigmoid(preact)
    grad_pre = (grad_act * sigma_pre * (1.0 + preact * (1.0 - sigma_pre))).astype(jnp.bfloat16)
    grad_low_up = dot_last(grad_pre, chosen_upward_raise)
    grad_mid_terms = dot_last(grad_pre, weight_upward) + dot_plain(
        grad_low_up, chosen_upward_lower.astype(jnp.float32)
    )
    delta_downward_lower = dot_first(grad_low_down, activated)
    delta_upward_raise = dot_first(low_upward, grad_pre)
    delta_upward_lower = dot_first(grad_low_up, mid_all.astype(jnp.float32))
    delta_downward_raise = dot_first(low_downward, grad_out_all.astype(jnp.float32))
    grad_mid = lax.psum_scatter(grad_mid_terms, "tensor", scatter_dimension=0, tiled=True)
    grad_middle = grad_out.astype(jnp.float32) + rms_back(grad_mid, unit_mid, factor_mid)
    grad_attn = grad_middle.astype(jnp.bfloat16)
    grad_attn_all = lax.all_gather(grad_attn, "tensor", axis=0, tiled=True)
    grad_low_out = dot_last(grad_attn_all, chosen_output_raise).astype(jnp.bfloat16)
    grad_attended = (
        dot_plain(grad_attn_all, weight_output) + dot_plain(grad_low_out, chosen_output_lower)
    ).astype(jnp.bfloat16)
    delta_output_lower = dot_first(grad_low_out, attended)
    delta_output_raise = dot_first(low_out, grad_attn_all.astype(jnp.float32))
    grad_heads = grad_attended.reshape(length, local_heads, HD)

    def backward_block(totals, block_index):
        grad_keys_acc, grad_values_acc = totals
        first_row = block_index * block_rows
        query_piece = lax.dynamic_slice_in_dim(queries, first_row, block_rows, 0)
        grad_piece = lax.dynamic_slice_in_dim(grad_heads, first_row, block_rows, 0)
        scores = masked_scores(query_piece, first_row)
        probabilities = jnp.exp(scores - log_totals[block_index][:, :, None])
        grad_probs = jnp.einsum(
            "qhd,khd->hqk", grad_piece, values_all, preferred_element_type=jnp.float32
        )
        row_dot = jnp.sum(probabilities * grad_probs, axis=-1, keepdims=True)
        grad_scores = (score_scale * probabilities * (grad_probs - row_dot)).astype(jnp.bfloat16)
        grad_query_piece = jnp.einsum(
            "hqk,khd->qhd", grad_scores, keys_all, preferred_element_type=jnp.float32
        ).astype(jnp.bfloat16)
        grad_keys_acc = grad_keys_acc + jnp.einsum(
            "hqk,qhd->khd", grad_scores, query_piece, preferred_element_type=jnp.float32
        )
        grad_values_acc = grad_values_acc + jnp.einsum(
            "hqk,qhd->khd",
            probabilities.astype(jnp.bfloat16),
            grad_piece,
            preferred_element_type=jnp.float32,
        )
        return ((grad_keys_acc, grad_values_acc), grad_query_piece)

    empty_heads = jnp.zeros((length, local_heads, HD), jnp.float32)
    (grad_keys_acc, grad_values_acc), grad_query_blocks = lax.scan(
        backward_block, (empty_heads, empty_heads), jnp.arange(block_count, dtype=jnp.int32)
    )
    grad_queries = grad_query_blocks.reshape(length, local_width)
    grad_keys = grad_keys_acc.astype(jnp.bfloat16).reshape(length, local_width)
    grad_values = grad_values_acc.astype(jnp.bfloat16).reshape(length, local_width)
    delta_query_raise = dot_first(low_query, grad_queries)
    delta_key_raise = dot_first(low_key, grad_keys)
    delta_value_raise = dot_first(low_value, grad_values)
    grad_low_qkv = jnp.concatenate(
        [
            dot_last(grad_queries, chosen_query_raise),
            dot_last(grad_keys, chosen_key_raise),
            dot_last(grad_values, chosen_value_raise),
        ],
        axis=1,
    )
    grad_in_terms = (
        dot_last(grad_queries, weight_query)
        + dot_last(grad_keys, weight_key)
        + dot_last(grad_values, weight_value)
    )
    grad_in_terms = grad_in_terms + dot_plain(grad_low_qkv, lower_qkv.astype(jnp.float32))
    delta_qkv = dot_first(grad_low_qkv, normed_all.astype(jnp.float32))
    grad_normed = lax.psum_scatter(
        grad_in_terms.astype(jnp.bfloat16), "tensor", scatter_dimension=0, tiled=True
    ).astype(jnp.float32)
    input_grad = (grad_middle + rms_back(grad_normed, unit_in, factor_in)).astype(jnp.bfloat16)
    summed_qkv, summed_up_lower, summed_out_raise, summed_down_raise = (
        lax.psum(delta_qkv.astype(jnp.bfloat16), "tensor").astype(jnp.float32),
        lax.psum(delta_upward_lower.astype(jnp.bfloat16), "tensor").astype(jnp.float32),
        lax.psum(delta_output_raise.astype(jnp.bfloat16), "tensor").astype(jnp.float32),
        lax.psum(delta_downward_raise.astype(jnp.bfloat16), "tensor").astype(jnp.float32),
    )
    delta_query_lower = summed_qkv[:adapter_rank]
    delta_key_lower = summed_qkv[adapter_rank : 2 * adapter_rank]
    delta_value_lower = summed_qkv[2 * adapter_rank :]
    choice_value = adapter_choice.astype(jnp.float32)
    set_numbers = jnp.arange(set_count, dtype=jnp.float32)
    members = (
        delta_query_lower,
        delta_query_raise,
        delta_key_lower,
        delta_key_raise,
        delta_value_lower,
        delta_value_raise,
        delta_output_lower,
        summed_out_raise,
        summed_up_lower,
        delta_upward_raise,
        delta_downward_lower,
        summed_down_raise,
    )
    empty_sets = tuple((jnp.zeros((set_count,) + member.shape, jnp.float32) for member in members))
    pieces = (
        lax.all_gather(
            delta_query_lower[None].astype(jnp.bfloat16), "dp", axis=0, tiled=True
        ).astype(jnp.float32),
        lax.all_gather(
            delta_query_raise[None].astype(jnp.bfloat16), "dp", axis=0, tiled=True
        ).astype(jnp.float32),
        lax.all_gather(delta_key_lower[None].astype(jnp.bfloat16), "dp", axis=0, tiled=True).astype(
            jnp.float32
        ),
        lax.all_gather(delta_key_raise[None].astype(jnp.bfloat16), "dp", axis=0, tiled=True).astype(
            jnp.float32
        ),
        lax.all_gather(
            delta_value_lower[None].astype(jnp.bfloat16), "dp", axis=0, tiled=True
        ).astype(jnp.float32),
        lax.all_gather(
            delta_value_raise[None].astype(jnp.bfloat16), "dp", axis=0, tiled=True
        ).astype(jnp.float32),
        lax.all_gather(
            delta_output_lower[None].astype(jnp.bfloat16), "dp", axis=0, tiled=True
        ).astype(jnp.float32),
        lax.all_gather(
            summed_out_raise[None].astype(jnp.bfloat16), "dp", axis=0, tiled=True
        ).astype(jnp.float32),
        lax.all_gather(summed_up_lower[None].astype(jnp.bfloat16), "dp", axis=0, tiled=True).astype(
            jnp.float32
        ),
        lax.all_gather(
            delta_upward_raise[None].astype(jnp.bfloat16), "dp", axis=0, tiled=True
        ).astype(jnp.float32),
        lax.all_gather(
            delta_downward_lower[None].astype(jnp.bfloat16), "dp", axis=0, tiled=True
        ).astype(jnp.float32),
        lax.all_gather(
            summed_down_raise[None].astype(jnp.bfloat16), "dp", axis=0, tiled=True
        ).astype(jnp.float32),
        lax.all_gather(choice_value.astype(jnp.bfloat16), "dp", axis=0, tiled=True).astype(
            jnp.float32
        ),
    )
    onehot_rows = (pieces[12][:, None] == set_numbers[None, :]).astype(jnp.float32)
    grads = tuple(
        (
            running
            + jnp.tensordot(onehot_rows, member, axes=((0,), (0,)), precision=FULL_PRECISION)
            for running, member in zip(empty_sets, pieces[:12])
        )
    )
    return (
        activations[None],
        input_grad[None],
        grads[0],
        grads[1],
        grads[2],
        grads[3],
        grads[4],
        grads[5],
        grads[6],
        grads[7],
        grads[8],
        grads[9],
        grads[10],
        grads[11],
    )


def solution(mesh):
    return jax.shard_map(
        on_device,
        mesh=mesh,
        in_specs=(
            P("dp", "tensor", None),
            P("dp", None),
            P("dp"),
            P("dp", "tensor", None),
            P(None, "tensor"),
            P(None, "tensor"),
            P(None, "tensor"),
            P(None, "tensor"),
            P(None, "tensor"),
            P(None, "tensor"),
            P(),
            P(None, None, "tensor"),
            P(),
            P(None, None, "tensor"),
            P(),
            P(None, None, "tensor"),
            P(None, None, "tensor"),
            P(),
            P(),
            P(None, None, "tensor"),
            P(None, None, "tensor"),
            P(),
        ),
        out_specs=(
            P("dp", "tensor", None),
            P("dp", "tensor", None),
            P(),
            P(None, None, "tensor"),
            P(),
            P(None, None, "tensor"),
            P(),
            P(None, None, "tensor"),
            P(None, None, "tensor"),
            P(),
            P(),
            P(None, None, "tensor"),
            P(None, None, "tensor"),
            P(),
        ),
        check_vma=False,
    )
```

profile of v0, /device:TPU:0, one launch (start us, length us, event | category | flops | bytes accessed | tf_op | source)
XLA Modules:
  0.0 1199.0 jit_solution(2146562869853011109)
XLA Ops:
  15.7 39.5 %all-gather.15.cloned.1.call-done = bf16[2048,1280]{1,0:T(8,128)(2,1)} async-done(((bf16[512,1280]{1,0:T(8,128)(2,1)}), bf16[2048,1280]{1,0:T(8,128)(2,1)}) %all-gather.15.cloned.1.call-update) | async-done | bytes 5242896 | tf_op jit(solution)/shard_map/all_gather | solution.py:95
  55.2 4.5 fusion.193
  70.9 72.9 %while.28 = (s32[]{:T(128)}, bf16[4,512,4,80]{1,3,2,0:T(8,128)(2,1)}, f32[4,4,512]{2,1,0:T(4,128)S(1)}, s32[4]{0:T(128)S(1)}, s32[2048]{0:T(1024)S(1)}, /*index=...) while((s32[]{:T(128)}, ...), condition=%wide.region_4.5_spmd.clone, body=%wide.region_1.4_spmd.clone.sunk | while | flops 1395816960 | bytes 63129840 | solution.py:134
  73.6 4.8 fusion.285
  78.5 4.5 fusion.286
  83.0 6.3 fusion.287
  91.8 4.8 fusion.285
  96.7 4.5 fusion.286
  101.2 6.3 fusion.287
  110.0 4.8 fusion.285
  114.8 4.5 fusion.286
  119.3 6.3 fusion.287
  128.1 4.8 fusion.285
  133.0 4.5 fusion.286
  137.5 6.3 fusion.287
  150.6 5.6 convolution_add_fusion.1
  157.4 84.2 %reduce-scatter.5.cloned.1.call-done = f32[512,1280]{1,0:T(8,128)} async-done(((f32[2048,1280]{1,0:T(8,128)}), f32[512,1280]{1,0:T(8,128)}) %reduce-scatter.5.cloned.1.call-update) | async-done | bytes 2621456 | tf_op jit(solution)/shard_map/reduce_scatter | solution.py:140
  250.2 33.4 %all-gather.21.cloned.1.call-done = bf16[1,2048,1280]{2,1,0:T(8,128)(2,1)} async-done(((bf16[1,512,1280]{2,1,0:T(8,128)(2,1)}), bf16[1,2048,1280]{2,1,0:T(8,128)(2,1)}) %all-gather.21.cloned.1.call-update) | async-done | bytes 5242896 | tf_op jit(solution)/shard_map/all_gather | solution.py:156
  287.8 4.6 fusion.46
  292.4 33.8 %all-gather.17.cloned.1.call-done = bf16[2048,1280]{1,0:T(8,128)(2,1)} async-done(((bf16[512,1280]{1,0:T(8,128)(2,1)}), bf16[2048,1280]{1,0:T(8,128)(2,1)}) %all-gather.17.cloned.1.call-update) | async-done | bytes 5242896 | tf_op jit(solution)/shard_map/all_gather | solution.py:146
  339.4 5.6 convolution_add_fusion
  345.0 85.4 %reduce-scatter.9.cloned.1.call-done = f32[512,1280]{1,0:T(8,128)} async-done(((f32[2048,1280]{1,0:T(8,128)}), f32[512,1280]{1,0:T(8,128)}) %reduce-scatter.9.cloned.1.call-update) | async-done | bytes 2621456 | tf_op jit(solution)/shard_map/reduce_scatter | solution.py:171
  444.2 4.5 fusion.71
  448.7 30.5 %all-gather.19.cloned.1.call-done = bf16[2048,1280]{1,0:T(8,128)(2,1)} async-done(((bf16[512,1280]{1,0:T(8,128)(2,1)}), bf16[2048,1280]{1,0:T(8,128)(2,1)}) %all-gather.19.cloned.1.call-update) | async-done | bytes 5242896 | tf_op jit(solution)/shard_map/all_gather | solution.py:174
  487.9 232.7 %while.29 = (s32[]{:T(128)}, f32[2048,4,80]{0,2,1:T(8,128)}, f32[2048,4,80]{0,2,1:T(8,128)}, bf16[4,512,4,80]{1,3,2,0:T(8,128)(2,1)}, s32[4]{0:T(128)S(1)}, /*in...) while((s32[]{:T(128)}, f32[2048,4,80]{0,2,1:T(8,128)}, ...), condition=%wide.region_12.13_spmd.clone, body=%wide.region_10.12_spmd.clone.sunk | while | flops 3428481536 | bytes 217459024 | solution.py:210
  496.8 5.8 copy-done.2
  502.6 7.8 fusion.300
  510.5 14.9 %multiply_reduce_fusion.4 = (f32[4,512]{1,0:T(4,128)S(1)}, f32[4,512,2048]{2,1,0:T(8,128)}) fusion(f32[4,512,2048]{2,1,0:T(8,128)} %copy-done.2, f32[4,512]{1,0:T(4,128)S(1)} %dynamic-slice_bitcast_fusion.2, pred[512,2048]{1,0:T(8,128)(4,1)} %fusion.298, bf16[2048,4,80]{0,2,1:T(8,128)(2,1)} %get-tuple-element.522, ...), kind=kOutput, calls=%fused_computation.21.clone.1 | convolution fusion | flops 692058112 | bytes 36257796 | tf_op jit(solution)/shard_map/while/body/eval_jaxpr/qhd,khd->hqk/dot_general | solution.py:190
  525.3 12.3 %multiply_convert_fusion.4 = bf16[4,512,2048]{2,1,0:T(8,128)(2,1)S(1)} fusion(f32[4,512,2048]{2,1,0:T(8,128)} %get-tuple-element.436, f32[4,512,2048]{2,1,0:T(8,128)} %copy-done.2, f32[4,512]{1,0:T(4,128)S(1)} %get-tuple-element.437, f32[4,512]{1,0:T(4,128)S(1)} %dynamic-slice_bitcast_fusion.2, pred[512,2048]{1,0:T(8,128)(4,1)S(1)} %copy-done.3), kind=kLoop, calls=%fused_computation.20.clone.1 | loop fusion | flops 29360128 | bytes 43008000 | tf_op jit(solution)/shard_map/while/body/eval_jaxpr/convert_element_type | solution.py:194
  541.1 4.1 fusion.299
  553.9 5.8 copy-done.2
  559.7 8.2 fusion.300
  568.0 14.9 %multiply_reduce_fusion.4 = (f32[4,512]{1,0:T(4,128)S(1)}, f32[4,512,2048]{2,1,0:T(8,128)}) fusion(f32[4,512,2048]{2,1,0:T(8,128)} %copy-done.2, f32[4,512]{1,0:T(4,128)S(1)} %dynamic-slice_bitcast_fusion.2, pred[512,2048]{1,0:T(8,128)(4,1)} %fusion.298, bf16[2048,4,80]{0,2,1:T(8,128)(2,1)} %get-tuple-element.522, ...), kind=kOutput, calls=%fused_computation.21.clone.1 | convolution fusion | flops 692058112 | bytes 36257796 | tf_op jit(solution)/shard_map/while/body/eval_jaxpr/qhd,khd->hqk/dot_general | solution.py:190
  582.9 12.3 %multiply_convert_fusion.4 = bf16[4,512,2048]{2,1,0:T(8,128)(2,1)S(1)} fusion(f32[4,512,2048]{2,1,0:T(8,128)} %get-tuple-element.436, f32[4,512,2048]{2,1,0:T(8,128)} %copy-done.2, f32[4,512]{1,0:T(4,128)S(1)} %get-tuple-element.437, f32[4,512]{1,0:T(4,128)S(1)} %dynamic-slice_bitcast_fusion.2, pred[512,2048]{1,0:T(8,128)(4,1)S(1)} %copy-done.3), kind=kLoop, calls=%fused_computation.20.clone.1 | loop fusion | flops 29360128 | bytes 43008000 | tf_op jit(solution)/shard_map/while/body/eval_jaxpr/convert_element_type | solution.py:194
  598.6 5.0 fusion.299
  612.4 5.8 copy-done.2
  618.2 8.2 fusion.300
  626.4 14.9 %multiply_reduce_fusion.4 = (f32[4,512]{1,0:T(4,128)S(1)}, f32[4,512,2048]{2,1,0:T(8,128)}) fusion(f32[4,512,2048]{2,1,0:T(8,128)} %copy-done.2, f32[4,512]{1,0:T(4,128)S(1)} %dynamic-slice_bitcast_fusion.2, pred[512,2048]{1,0:T(8,128)(4,1)} %fusion.298, bf16[2048,4,80]{0,2,1:T(8,128)(2,1)} %get-tuple-element.522, ...), kind=kOutput, calls=%fused_computation.21.clone.1 | convolution fusion | flops 692058112 | bytes 36257796 | tf_op jit(solution)/shard_map/while/body/eval_jaxpr/qhd,khd->hqk/dot_general | solution.py:190
  641.3 12.3 %multiply_convert_fusion.4 = bf16[4,512,2048]{2,1,0:T(8,128)(2,1)S(1)} fusion(f32[4,512,2048]{2,1,0:T(8,128)} %get-tuple-element.436, f32[4,512,2048]{2,1,0:T(8,128)} %copy-done.2, f32[4,512]{1,0:T(4,128)S(1)} %get-tuple-element.437, f32[4,512]{1,0:T(4,128)S(1)} %dynamic-slice_bitcast_fusion.2, pred[512,2048]{1,0:T(8,128)(4,1)S(1)} %copy-done.3), kind=kLoop, calls=%fused_computation.20.clone.1 | loop fusion | flops 29360128 | bytes 43008000 | tf_op jit(solution)/shard_map/while/body/eval_jaxpr/convert_element_type | solution.py:194
  657.0 5.0 fusion.299
  670.7 5.8 copy-done.2
  676.5 8.2 fusion.300
  684.8 14.9 %multiply_reduce_fusion.4 = (f32[4,512]{1,0:T(4,128)S(1)}, f32[4,512,2048]{2,1,0:T(8,128)}) fusion(f32[4,512,2048]{2,1,0:T(8,128)} %copy-done.2, f32[4,512]{1,0:T(4,128)S(1)} %dynamic-slice_bitcast_fusion.2, pred[512,2048]{1,0:T(8,128)(4,1)} %fusion.298, bf16[2048,4,80]{0,2,1:T(8,128)(2,1)} %get-tuple-element.522, ...), kind=kOutput, calls=%fused_computation.21.clone.1 | convolution fusion | flops 692058112 | bytes 36257796 | tf_op jit(solution)/shard_map/while/body/eval_jaxpr/qhd,khd->hqk/dot_general | solution.py:190
  699.7 12.3 %multiply_convert_fusion.4 = bf16[4,512,2048]{2,1,0:T(8,128)(2,1)S(1)} fusion(f32[4,512,2048]{2,1,0:T(8,128)} %get-tuple-element.436, f32[4,512,2048]{2,1,0:T(8,128)} %copy-done.2, f32[4,512]{1,0:T(4,128)S(1)} %get-tuple-element.437, f32[4,512]{1,0:T(4,128)S(1)} %dynamic-slice_bitcast_fusion.2, pred[512,2048]{1,0:T(8,128)(4,1)S(1)} %copy-done.3), kind=kLoop, calls=%fused_computation.20.clone.1 | loop fusion | flops 29360128 | bytes 43008000 | tf_op jit(solution)/shard_map/while/body/eval_jaxpr/convert_element_type | solution.py:194
  715.4 5.0 fusion.299
  723.0 5.6 fusion.201
  730.9 5.5 fusion.200
  738.6 5.5 fusion.199
  745.7 4.1 convolution_convert_fusion.1
  749.9 13.5 %add_convert_fusion = bf16[2048,1280]{1,0:T(8,128)(2,1)} fusion(f32[2048,1280]{1,0:T(8,128)} %fusion.201, f32[2048,1280]{1,0:T(8,128)} %fusion.199, f32[2048,1280]{1,0:T(8,128)} %fusion.200, bf16[2048,16]{0,1:T(8,128)(2,1)S(1)} %fusion.132, bf16[2048,16]{0,1:T(8,128)(2,1)S(1)} %fusion.131, bf16[2048,16]{0,1:T(8,128)(2,1)S(1)} %fusion.130, ...), kind=kOutput, calls=%fused_computation.49 | convolution fusion | flops 263102464 | bytes 37019648 | tf_op jit(solution)/shard_map/dot_general | solution.py:36
  774.5 21.3 %all-reduce = bf16[8]{0:T(256)(128)(2,1)S(1)} all-reduce(bf16[8]{0:T(256)(128)(2,1)S(1)} %dynamic-update-slice), channel_id=1, replica_groups=mesh['dp'=8,'tensor'=4] {'dp'}, use_global_device_ids=true, to_apply=%add | all-reduce | flops 8 | bytes 32
  797.7 30.7 %all-gather.9 = bf16[128,320]{1,0:T(8,128)(2,1)S(1)} all-gather(bf16[16,320]{1,0:T(8,128)(2,1)S(1)} %convolution_convert_fusion.7), channel_id=11, replica_groups=mesh['dp'=8,'tensor'=4] {'dp'}, dimensions={0}, use_global_device_ids=true | all-gather | bytes 92160 | tf_op jit(solution)/shard_map/all_gather | solution.py:295
  831.0 30.7 %all-gather.8 = bf16[128,320]{1,0:T(8,128)(2,1)S(1)} all-gather(bf16[16,320]{1,0:T(8,128)(2,1)S(1)} %convolution_convert_fusion.8), channel_id=10, replica_groups=mesh['dp'=8,'tensor'=4] {'dp'}, dimensions={0}, use_global_device_ids=true | all-gather | bytes 92160 | tf_op jit(solution)/shard_map/all_gather | solution.py:292
  863.0 30.6 %all-gather.7 = bf16[128,320]{1,0:T(8,128)(2,1)S(1)} all-gather(bf16[16,320]{1,0:T(8,128)(2,1)S(1)} %convolution_convert_fusion.9), channel_id=9, replica_groups=mesh['dp'=8,'tensor'=4] {'dp'}, dimensions={0}, use_global_device_ids=true | all-gather | bytes 92160 | tf_op jit(solution)/shard_map/all_gather | solution.py:283
  894.8 30.6 %all-gather.2 = bf16[128,320]{1,0:T(8,128)(2,1)S(1)} all-gather(bf16[16,320]{1,0:T(8,128)(2,1)S(1)} %convolution_convert_fusion.12), channel_id=4, replica_groups=mesh['dp'=8,'tensor'=4] {'dp'}, dimensions={0}, use_global_device_ids=true | all-gather | bytes 92160 | tf_op jit(solution)/shard_map/all_gather | solution.py:268
  926.7 30.6 %all-gather.4 = bf16[128,320]{1,0:T(8,128)(2,1)S(1)} all-gather(bf16[16,320]{1,0:T(8,128)(2,1)S(1)} %convolution_convert_fusion.11), channel_id=6, replica_groups=mesh['dp'=8,'tensor'=4] {'dp'}, dimensions={0}, use_global_device_ids=true | all-gather | bytes 92160 | tf_op jit(solution)/shard_map/all_gather | solution.py:274
  958.6 30.7 %all-gather.6 = bf16[128,320]{1,0:T(8,128)(2,1)S(1)} all-gather(bf16[16,320]{1,0:T(8,128)(2,1)S(1)} %convolution_convert_fusion.10), channel_id=8, replica_groups=mesh['dp'=8,'tensor'=4] {'dp'}, dimensions={0}, use_global_device_ids=true | all-gather | bytes 92160 | tf_op jit(solution)/shard_map/all_gather | solution.py:280
  990.1 31.2 %all_gather.63 = bf16[8,16,1280]{2,1,0:T(8,128)(2,1)S(1)} all-gather(bf16[1,16,1280]{2,1,0:T(8,128)(2,1)} %get-tuple-element.286), channel_id=1, replica_groups=mesh['dp'=8,'tensor'=4] {'dp'}, dimensions={0}, use_global_device_ids=true | all-gather | bytes 368640 | tf_op jit(solution)/shard_map/all_gather | solution.py:286
  1022.6 30.8 %all_gather.64 = bf16[8,16,1280]{2,1,0:T(8,128)(2,1)S(1)} all-gather(bf16[1,16,1280]{2,1,0:T(8,128)(2,1)S(1)} %copy-done.73), channel_id=1, replica_groups=mesh['dp'=8,'tensor'=4] {'dp'}, dimensions={0}, use_global_device_ids=true | all-gather | bytes 368640 | tf_op jit(solution)/shard_map/all_gather | solution.py:289
  1054.7 30.9 %all_gather.67 = bf16[8,16,1280]{2,1,0:T(8,128)(2,1)S(1)} all-gather(bf16[1,16,1280]{2,1,0:T(8,128)(2,1)S(1)} %copy-done.72), channel_id=1, replica_groups=mesh['dp'=8,'tensor'=4] {'dp'}, dimensions={0}, use_global_device_ids=true | all-gather | bytes 368640 | tf_op jit(solution)/shard_map/all_gather | solution.py:298
  1087.8 30.9 %all-gather.5 = bf16[128,1280]{1,0:T(8,128)(2,1)S(1)} all-gather(bf16[16,1280]{1,0:T(8,128)(2,1)S(1)} %get-tuple-element.295), channel_id=7, replica_groups=mesh['dp'=8,'tensor'=4] {'dp'}, dimensions={0}, use_global_device_ids=true | all-gather | bytes 368640 | tf_op jit(solution)/shard_map/all_gather | solution.py:277
  1119.9 31.0 %all-gather.3 = bf16[128,1280]{1,0:T(8,128)(2,1)S(1)} all-gather(bf16[16,1280]{1,0:T(8,128)(2,1)S(1)} %get-tuple-element.296), channel_id=5, replica_groups=mesh['dp'=8,'tensor'=4] {'dp'}, dimensions={0}, use_global_device_ids=true | all-gather | bytes 368640 | tf_op jit(solution)/shard_map/all_gather | solution.py:271
  1152.2 31.0 %all-gather.1 = bf16[128,1280]{1,0:T(8,128)(2,1)S(1)} all-gather(bf16[16,1280]{1,0:T(8,128)(2,1)S(1)} %get-tuple-element.297), channel_id=3, replica_groups=mesh['dp'=8,'tensor'=4] {'dp'}, dimensions={0}, use_global_device_ids=true | all-gather | bytes 368640 | tf_op jit(solution)/shard_map/all_gather | solution.py:265
  1186.4 5.3 fusion.75
  (350 shorter events, 160.6 us)
Async XLA Ops:
  7.2 323.0 %copy-start = (bf16[1280,320]{0,1:T(8,128)(2,1)S(1)}, bf16[1280,320]{0,1:T(8,128)(2,1)}, u32[]{:S(2)}) copy-start(bf16[1280,320]{0,1:T(8,128)(2,1)} %param.34) | copy-start | bytes 2457604
  7.2 5.4 copy-start.51
  7.2 5.7 copy-start.64
  7.2 48.0 %all-gather.15.cloned.1.call-start = ((), (), s32[]{:S(2)}) async-start(), calls=%async_computation.4 | async-start | bytes 6553600 | tf_op jit(solution)/shard_map/all_gather | solution.py:95
  9.0 4.4 copy-start.67
  9.0 5.2 copy-start.52
  9.1 6.1 copy-start.53
  9.1 6.3 copy-start.54
  9.1 46.1 %copy-start.27 = (bf16[1280,320]{0,1:T(8,128)(2,1)S(1)}, bf16[1280,320]{0,1:T(8,128)(2,1)}, u32[]{:S(2)}) copy-start(bf16[1280,320]{0,1:T(8,128)(2,1)} %param.32) | copy-start | bytes 2457604
  11.9 229.7 %reduce-scatter.5.cloned.1.call-start = ((), (), s32[]{:S(2)}) async-start(), calls=%async_computation.5 | async-start | bytes 13107200 | tf_op jit(solution)/shard_map/reduce_scatter | solution.py:140
  12.9 46.8 %copy-start.40 = (bf16[1,16,1280]{2,1,0:T(8,128)(2,1)}, bf16[1,16,1280]{2,1,0:T(8,128)(2,1)S(1)}, u32[]{:S(2)}) copy-start(bf16[1,16,1280]{2,1,0:T(8,128)(2,1)S(1)} %copy.218) | copy-start | bytes 122884
  13.1 55.0 %copy-start.57 = (bf16[1,16,320]{2,0,1:T(2,128)(2,1)}, bf16[1,16,320]{2,0,1:T(2,128)(2,1)S(1)}, u32[]{:S(2)}) copy-start(bf16[1,16,320]{2,0,1:T(2,128)(2,1)S(1)} %fusion.110) | copy-start | bytes 30724
  13.3 51.8 %copy-start.59 = (bf16[1,16,320]{2,0,1:T(2,128)(2,1)}, bf16[1,16,320]{2,0,1:T(2,128)(2,1)S(1)}, u32[]{:S(2)}) copy-start(bf16[1,16,320]{2,0,1:T(2,128)(2,1)S(1)} %fusion.108) | copy-start | bytes 30724
  13.5 48.0 %copy-start.61 = (bf16[1,16,320]{2,0,1:T(2,128)(2,1)}, bf16[1,16,320]{2,0,1:T(2,128)(2,1)S(1)}, u32[]{:S(2)}) copy-start(bf16[1,16,320]{2,0,1:T(2,128)(2,1)S(1)} %fusion.106) | copy-start | bytes 30724
  15.6 44.1 %copy-start.42 = (bf16[16,1280]{1,0:T(8,128)(2,1)}, bf16[16,1280]{1,0:T(8,128)(2,1)S(1)}, u32[]{:S(2)}) copy-start(bf16[16,1280]{1,0:T(8,128)(2,1)S(1)} %get-tuple-element.300) | copy-start | bytes 122884
  15.7 44.1 %copy-start.44 = (bf16[16,1280]{1,0:T(8,128)(2,1)}, bf16[16,1280]{1,0:T(8,128)(2,1)S(1)}, u32[]{:S(2)}) copy-start(bf16[16,1280]{1,0:T(8,128)(2,1)S(1)} %get-tuple-element.301) | copy-start | bytes 122884
  55.2 4.6 copy-start.10
  61.4 6.7 copy-start.23
  78.5 4.5 copy-start.7
  96.7 4.5 copy-start.7
  114.8 4.5 copy-start.7
  133.0 4.5 copy-start.7
  156.2 127.5 %all-gather.21.cloned.1.call-start = ((), (), s32[]{:S(2)}) async-start(), calls=%async_computation.12 | async-start | bytes 6553600 | tf_op jit(solution)/shard_map/all_gather | solution.py:156
  156.9 169.2 %all-gather.17.cloned.1.call-start = ((), (), s32[]{:S(2)}) async-start(), calls=%async_computation.6 | async-start | bytes 6553600 | tf_op jit(solution)/shard_map/all_gather | solution.py:146
  244.6 189.5 %copy-start.70 = (f32[512]{0:T(512)}, f32[512]{0:T(512)S(1)}, u32[]{:S(2)}) copy-start(f32[512]{0:T(512)S(1)} %add_rsqrt_fusion) | copy-start | bytes 6148
  247.4 183.1 %reduce-scatter.9.cloned.1.call-start = ((), (), s32[]{:S(2)}) async-start(), calls=%async_computation.8 | async-start | bytes 13107200 | tf_op jit(solution)/shard_map/reduce_scatter | solution.py:171
  250.2 37.6 %copy-start.48 = (bf16[1,16,1280]{2,0,1:T(2,128)(2,1)}, bf16[1,16,1280]{2,0,1:T(2,128)(2,1)S(1)}, u32[]{:S(2)}) copy-start(bf16[1,16,1280]{2,0,1:T(2,128)(2,1)S(1)} %fusion.76) | copy-start | bytes 122884
  287.8 46.3 %copy-start.55 = (bf16[16,2048]{1,0:T(8,128)(2,1)}, bf16[16,2048]{1,0:T(8,128)(2,1)S(1)}, u32[]{:S(2)}) copy-start(bf16[16,2048]{1,0:T(8,128)(2,1)S(1)} %fusion.66) | copy-start | bytes 196612
  345.0 134.2 %all-gather.19.cloned.1.call-start = ((), (), s32[]{:S(2)}) async-start(), calls=%async_computation.9 | async-start | bytes 6553600 | tf_op jit(solution)/shard_map/all_gather | solution.py:174
  430.4 4.5 copy-start.11
  438.6 551.6 %all-reduce.7.cloned.1.call-start = ((), (), s32[]{:S(2)}) async-start(), calls=%async_computation.13 | async-start | bytes 245760 | tf_op jit(solution)/shard_map/psum | solution.py:241
  496.8 5.8 copy-start.2
  510.5 14.9 %copy-start.3 = (pred[512,2048]{1,0:T(8,128)(4,1)S(1)}, pred[512,2048]{1,0:T(8,128)(4,1)}, u32[]{:S(2)}) copy-start(pred[512,2048]{1,0:T(8,128)(4,1)} %fusion.298) | copy-start | bytes 3145732 | tf_op jit(solution)/shard_map/while
  553.9 5.8 copy-start.2
  568.0 14.9 %copy-start.3 = (pred[512,2048]{1,0:T(8,128)(4,1)S(1)}, pred[512,2048]{1,0:T(8,128)(4,1)}, u32[]{:S(2)}) copy-start(pred[512,2048]{1,0:T(8,128)(4,1)} %fusion.298) | copy-start | bytes 3145732 | tf_op jit(solution)/shard_map/while
  612.4 5.8 copy-start.2
  626.4 14.9 %copy-start.3 = (pred[512,2048]{1,0:T(8,128)(4,1)S(1)}, pred[512,2048]{1,0:T(8,128)(4,1)}, u32[]{:S(2)}) copy-start(pred[512,2048]{1,0:T(8,128)(4,1)} %fusion.298) | copy-start | bytes 3145732 | tf_op jit(solution)/shard_map/while
  670.7 5.8 copy-start.2
  684.8 14.9 %copy-start.3 = (pred[512,2048]{1,0:T(8,128)(4,1)S(1)}, pred[512,2048]{1,0:T(8,128)(4,1)}, u32[]{:S(2)}) copy-start(pred[512,2048]{1,0:T(8,128)(4,1)} %fusion.298) | copy-start | bytes 3145732 | tf_op jit(solution)/shard_map/while
  730.6 5.8 copy-start.14
  730.9 5.5 copy-start.22
  737.8 6.3 copy-start.16
  737.8 6.3 slice-start
  738.6 5.5 slice-start.1
  738.6 5.5 copy-start.37
  745.6 341.3 %all-reduce.5.cloned.1.call-start = ((), (), s32[]{:S(2)}) async-start(), calls=%async_computation.11 | async-start | bytes 245760 | tf_op jit(solution)/shard_map/psum | solution.py:239
  749.8 434.6 %reduce-scatter.11.cloned.1.call-start = ((), (), s32[]{:S(2)}) async-start(), calls=%async_computation.10 | async-start | bytes 6553600 | tf_op jit(solution)/shard_map/reduce_scatter | solution.py:234
  763.4 4.5 copy-start.39
  763.5 422.9 %reduce-scatter.7.cloned.1.call-start = ((), (), s32[]{:S(2)}) async-start(), calls=%async_computation.7 | async-start | bytes 6553600 | tf_op jit(solution)/shard_map/reduce_scatter | solution.py:152
  771.9 24.0 %copy-start.56 = (bf16[16,2048]{1,0:T(8,128)(2,1)S(1)}, bf16[16,2048]{1,0:T(8,128)(2,1)}, u32[]{:S(2)}) copy-start(bf16[16,2048]{1,0:T(8,128)(2,1)} %copy-done.55) | copy-start | bytes 196612
  771.9 57.3 %copy-start.47 = (bf16[2048,16]{0,1:T(8,128)(2,1)S(1)}, bf16[2048,16]{0,1:T(8,128)(2,1)}, u32[]{:S(2)}) copy-start(bf16[2048,16]{0,1:T(8,128)(2,1)} %copy-done.46) | copy-start | bytes 196612
  771.9 90.6 %copy-start.13 = (bf16[40,8,4,512]{3,1,2,0:T(8,128)(2,1)S(1)}, bf16[40,8,4,512]{3,1,2,0:T(8,128)(2,1)}, u32[]{:S(2)}) copy-start(bf16[40,8,4,512]{3,1,2,0:T(8,128)(2,1)} %copy-done.12) | copy-start | bytes 3932164
  771.9 90.6 %copy-start.35 = (bf16[2048,16]{0,1:T(8,128)(2,1)S(1)}, bf16[2048,16]{0,1:T(8,128)(2,1)}, u32[]{:S(2)}) copy-start(bf16[2048,16]{0,1:T(8,128)(2,1)} %copy-done.34) | copy-start | bytes 196612
  797.6 96.7 %copy-start.17 = (bf16[40,8,4,512]{3,1,2,0:T(8,128)(2,1)S(1)}, bf16[40,8,4,512]{3,1,2,0:T(8,128)(2,1)}, u32[]{:S(2)}) copy-start(bf16[40,8,4,512]{3,1,2,0:T(8,128)(2,1)} %copy-done.16) | copy-start | bytes 3932164
  797.6 96.7 %copy-start.24 = (bf16[2048,48]{0,1:T(8,128)(2,1)S(1)}, bf16[2048,48]{0,1:T(8,128)(2,1)}, u32[]{:S(2)}) copy-start(bf16[2048,48]{0,1:T(8,128)(2,1)} %copy-done.23) | copy-start | bytes 589828
  831.0 95.3 %copy-start.15 = (bf16[2048,4,80]{0,2,1:T(8,128)(2,1)S(1)}, bf16[2048,4,80]{0,2,1:T(8,128)(2,1)}, u32[]{:S(2)}) copy-start(bf16[2048,4,80]{0,2,1:T(8,128)(2,1)} %copy-done.14) | copy-start | bytes 3932164
  990.1 32.5 %copy-start.73 = (bf16[1,16,1280]{2,1,0:T(8,128)(2,1)S(1)}, bf16[1,16,1280]{2,1,0:T(8,128)(2,1)}, u32[]{:S(2)}) copy-start(bf16[1,16,1280]{2,1,0:T(8,128)(2,1)} %get-tuple-element.287) | copy-start | bytes 122884
  990.1 64.6 %copy-start.72 = (bf16[1,16,1280]{2,1,0:T(8,128)(2,1)S(1)}, bf16[1,16,1280]{2,1,0:T(8,128)(2,1)}, u32[]{:S(2)}) copy-start(bf16[1,16,1280]{2,1,0:T(8,128)(2,1)} %get-tuple-element.288) | copy-start | bytes 122884
  1119.9 64.5 %copy-start.4 = (bf16[1,512,1280]{2,1,0:T(8,128)(2,1)S(1)}, bf16[1,512,1280]{2,1,0:T(8,128)(2,1)}, u32[]{:S(2)}) copy-start(bf16[1,512,1280]{2,1,0:T(8,128)(2,1)} %param.26) | copy-start | bytes 3932164
  1119.9 64.5 %copy-start.75 = (f32[512]{0:T(512)S(1)}, f32[512]{0:T(512)}, u32[]{:S(2)}) copy-start(f32[512]{0:T(512)} %copy-done.74) | copy-start | bytes 6148
  1152.2 34.2 %copy-start.21 = (bf16[1,512,1280]{2,1,0:T(8,128)(2,1)S(1)}, bf16[1,512,1280]{2,1,0:T(8,128)(2,1)}, u32[]{:S(2)}) copy-start(bf16[1,512,1280]{2,1,0:T(8,128)(2,1)} %param.29) | copy-start | bytes 3932164
  1152.2 34.2 %copy-start.71 = (f32[512]{0:T(512)S(1)}, f32[512]{0:T(512)}, u32[]{:S(2)}) copy-start(f32[512]{0:T(512)} %copy-done.70) | copy-start | bytes 6148
  1152.2 34.2 %copy-start.77 = (f32[512]{0:T(512)S(1)}, f32[512]{0:T(512)}, u32[]{:S(2)}) copy-start(f32[512]{0:T(512)} %copy-done.76) | copy-start | bytes 6148
  1186.4 5.3 copy-start.1
  (37 other events, 98.9 us)
Sparse Core Ops, SparseCore 0:
  12.0 43.1 all-gather.14
  156.3 85.2 reduce-scatter.4
  243.2 40.4 all-gather.20
  285.7 40.4 all-gather.16
  345.1 85.2 reduce-scatter.8
  438.7 40.4 all-gather.18
  745.7 30.9 all-reduce.6
  779.7 31.2 all-reduce.4
  813.5 52.0 reduce-scatter.10
  868.1 51.3 reduce-scatter.6
where the time goes:
time: 1210 us; the launch traced here: 1200 us
  blocking collectives  391 us (32%)
  waiting for transfers between devices  308 us (25%)
  matrix products  306 us (25%)
  other arithmetic  109 us (9%)
  local copies, waits for them, and re-layouts  53.7 us (4%)
  between operations  16.8 us (1%)
  loops' own time  13.6 us (1%)
    reduce_scatter x1, waiting for transfers between devices, on_device(): lax.psum_scatter(grad_mid_terms, 'tensor', scatter_dimension=0, tiled=True)  85.4 us
    reduce_scatter x1, waiting for transfers between devices, on_device(): lax.psum_scatter(attn_terms, 'tensor', scatter_dimension=0, tiled=True)  84.2 us
    dot_general x4, matrix products, backward_block(): jnp.einsum('qhd,khd->hqk', grad_piece, values_all, preferred_element_type...  59.6 us
    dot_general x16, matrix products, dot_plain(): return jnp.dot(left, right, preferred_element_type=jnp.float32)  53.8 us
    convert_element_type x4, other arithmetic, backward_block(): (score_scale * probabilities * (grad_probs - row_dot)).astype(jnp.bfloat16)  49.3 us
    dot_general x16, matrix products, dot_last(): lax.dot_general(left, right, (((1,), (1,)), ((), ())), preferred_element_...  42.5 us
    all_gather x1, waiting for transfers between devices, on_device(): normed_all = lax.all_gather(normed_in, 'tensor', axis=0, tiled=True)  39.5 us
    all_gather x1, waiting for transfers between devices, on_device(): mid_all = lax.all_gather(normed_mid, 'tensor', axis=0, tiled=True)  33.8 us
  transfers between devices with their start and end apart: 10, of which 6 were waited for; matrix products, arithmetic and copies ran while one was open for 6% of the time, Pallas kernels for 0%

commit v1 on v0

v1 whole, which is shorter than its diff:
```python
import functools
import math

import jax
import jax.numpy as jnp
from jax import lax
from jax.experimental import pallas as pl
from jax.experimental.pallas import tpu as pltpu
from jax.sharding import PartitionSpec as P

HD = 80
LANES = 128
EPS = 1e-06
NEG = -1e30
F32 = jnp.float32
BF16 = jnp.bfloat16
VMEM_BYTES = 60 * 2**20
SCORE_SCALE = HD ** (-0.5)
LOG2E = math.log2(math.e)
SLOT = 384

NT = (((1,), (1,)), ((), ()))
TN = (((0,), (0,)), ((), ()))


def nn(left, right):
    return jnp.dot(left, right, preferred_element_type=F32)


def nt(left, right):
    return lax.dot_general(left, right, NT, preferred_element_type=F32)


def tn(left, right):
    return lax.dot_general(left, right, TN, preferred_element_type=F32)


def params(**more):
    return pltpu.CompilerParams(vmem_limit_bytes=VMEM_BYTES, **more)


def cost(flops, nbytes):
    return pl.CostEstimate(flops=int(flops), bytes_accessed=int(nbytes), transcendentals=0)


def whole(shape):
    return pl.BlockSpec(shape, lambda *_: (0,) * len(shape))


def swap(array, axis_name, count, bit):
    return lax.ppermute(array, axis_name, [(i, i ^ bit) for i in range(count)])


def norm_kernel(choice, x_ref, ol_ref, ur_ref, dl_ref, out_ref):
    rows = x_ref.shape[0]
    x = x_ref[...].astype(F32)
    factor = lax.rsqrt(jnp.mean(x * x, axis=-1, keepdims=True) + EPS)
    out_ref[:rows] = (x * factor).astype(BF16)
    out_ref[rows:] = jnp.zeros_like(out_ref[rows:])
    width = ol_ref.shape[2]
    for slot, ref in enumerate((ol_ref, ur_ref, dl_ref)):
        out_ref[rows:, slot * SLOT : slot * SLOT + width] = ref[0]


def norm_call(x, choice, ol, ur, dl):
    rows, width = x.shape
    rank, local = ol.shape[1:]
    pick = pl.BlockSpec((1, rank, local), lambda g, c: (c[0], 0, 0))
    return pl.pallas_call(
        norm_kernel,
        grid_spec=pltpu.PrefetchScalarGridSpec(
            num_scalar_prefetch=1,
            grid=(1,),
            in_specs=[whole((rows, width)), pick, pick, pick],
            out_specs=whole((rows + rank, width)),
        ),
        out_shape=jax.ShapeDtypeStruct((rows + rank, width), BF16),
        compiler_params=params(),
        name="norm_in",
    )(choice, x, ol, ur, dl)


def prep_kernel(heads, wq, wk, wv, wo, wu, wd, pq, pk, pv, wt):
    for src, dst in ((wq, pq), (wk, pk), (wv, pv)):
        value = src[...].astype(F32)
        for h in range(heads):
            piece = value[:, h * HD : (h + 1) * HD]
            piece = jnp.concatenate(
                [piece, jnp.zeros((piece.shape[0], LANES - HD), F32)], axis=1
            )
            dst[:, h * LANES : (h + 1) * LANES] = piece.astype(BF16)
    width = wo.shape[1]
    for n, src in enumerate((wo, wu, wd)):
        wt[n * width : (n + 1) * width] = src[...].astype(F32).T.astype(BF16)


def prep_call(wq, wk, wv, wo, wu, wd):
    depth, width = wq.shape
    heads = width // HD
    step = 256
    src = pl.BlockSpec((step, width), lambda g: (g, 0))
    dst = pl.BlockSpec((step, heads * LANES), lambda g: (g, 0))
    padded = jax.ShapeDtypeStruct((depth, heads * LANES), BF16)
    return pl.pallas_call(
        functools.partial(prep_kernel, heads),
        grid=(depth // step,),
        in_specs=[src] * 6,
        out_specs=[dst, dst, dst, pl.BlockSpec((3 * width, step), lambda g: (0, g))],
        out_shape=[padded, padded, padded, jax.ShapeDtypeStruct((3 * width, depth), BF16)],
        compiler_params=params(),
        name="weight_layouts",
    )(wq, wk, wv, wo, wu, wd)


def pad_heads(value, heads):
    parts = []
    for h in range(heads):
        parts.append(value[:, h * HD : (h + 1) * HD])
        parts.append(jnp.zeros((value.shape[0], LANES - HD), value.dtype))
    return jnp.concatenate(parts, axis=1)


def qkv_kernel(
    heads, scal, p0, p1, p2, p3, wq, wk, wv, lq, lk, lv, rq, rk, rv,
    q_ref, k_ref, v_ref, kt_ref, vt_ref, low_ref, buf, sems,
):
    x = pl.program_id(0)
    rows = buf.shape[1]
    pieces = (p0, p1, p2, p3)
    copies = [
        pltpu.make_async_copy(pieces[n].at[pl.ds(0, rows)], buf.at[n], sems.at[n])
        for n in range(4)
    ]

    @pl.when(x == 0)
    def _():
        for c in copies:
            c.start()

    for n in range(4):

        @pl.when(x == n)
        def _(n=n):
            copies[n].wait()

    block = buf[x]
    lower = jnp.concatenate([lq[0], lk[0], lv[0]], axis=0)
    low = nt(block, lower).astype(BF16)
    low_ref[...] = low
    rank = lq.shape[1]
    for n, (w, r, row_ref, col_ref) in enumerate(
        ((wq, rq, q_ref, None), (wk, rk, k_ref, kt_ref), (wv, rv, v_ref, vt_ref))
    ):
        raise_pad = pad_heads(r[0].astype(F32), heads).astype(BF16)
        out = nn(block, w[...]) + nn(low[:, n * rank : (n + 1) * rank], raise_pad)
        if n == 0:
            out = out * (SCORE_SCALE * LOG2E)
        row_ref[...] = out.astype(BF16)
        if col_ref is not None:
            col_ref[...] = out.T.astype(BF16)


def qkv_call(scal, pieces, padded, lowers, raises, rows, length):
    depth, wide = padded[0].shape
    heads = wide // LANES
    rank = lowers[0].shape[1]
    width = raises[0].shape[2]
    any_spec = pl.BlockSpec(memory_space=pl.ANY)
    lower = pl.BlockSpec((1, rank, depth), lambda g, s: (s[0], 0, 0))
    raise_ = pl.BlockSpec((1, rank, width), lambda g, s: (s[0], 0, 0))
    row = pl.BlockSpec((rows, wide), lambda g, s: (s[1] ^ g, 0))
    col = pl.BlockSpec((wide, rows), lambda g, s: (0, s[1] ^ g))
    low = pl.BlockSpec((rows, 3 * rank), lambda g, s: (s[1] ^ g, 0))
    row_t = jax.ShapeDtypeStruct((length, wide), BF16)
    col_t = jax.ShapeDtypeStruct((wide, length), BF16)
    return pl.pallas_call(
        functools.partial(qkv_kernel, heads),
        grid_spec=pltpu.PrefetchScalarGridSpec(
            num_scalar_prefetch=1,
            grid=(4,),
            in_specs=[any_spec] * 4 + [whole((depth, wide))] * 3 + [lower] * 3 + [raise_] * 3,
            out_specs=[row, row, row, col, col, low],
            scratch_shapes=[
                pltpu.VMEM((4, rows, depth), BF16),
                pltpu.SemaphoreType.DMA((4,)),
            ],
        ),
        out_shape=[
            row_t, row_t, row_t, col_t, col_t,
            jax.ShapeDtypeStruct((length, 3 * rank), BF16),
        ],
        compiler_params=params(),
        cost_estimate=cost(2 * length * depth * wide * 3, 12 * length * wide),
        name="project",
    )(scal, *pieces, *padded, *lowers, *raises)


def allowed_mask(seg_row, seg_col, first, last, start, size):
    ok = seg_col[first:last, :] == seg_row[:, start : start + size]
    if last > start:
        key = lax.broadcasted_iota(jnp.int32, (last - first, size), 0) + first
        query = lax.broadcasted_iota(jnp.int32, (last - first, size), 1) + start
        ok = ok & (key <= query)
    return ok


def attend_kernel(
    step, scal, seg_row, seg_col, q_ref, k_ref, vt_ref,
    ot_ref, lse_ref, o0, o1, o2, o3, wide,
):
    h = pl.program_id(0)
    length = q_ref.shape[0]
    for i in range(length // step):
        start, last = i * step, (i + 1) * step
        s = nt(k_ref[:last], q_ref[start:last])
        s = jnp.where(allowed_mask(seg_row, seg_col, 0, last, start, step), s, NEG)
        top = jnp.max(s, axis=0, keepdims=True)
        p = jnp.exp2(s - top)
        total = jnp.sum(p, axis=0, keepdims=True)
        out = nn(vt_ref[:HD, :last], p.astype(BF16)) / total
        ot_ref[:, start:last] = out.astype(BF16)
        wide[pl.ds(pl.multiple_of(h * HD, 16), HD), start:last] = out
        lse_ref[0, :, start:last] = top + jnp.log2(total)

    @pl.when(h == pl.num_programs(0) - 1)
    def _():
        rows = o0.shape[0]
        for x, ref in enumerate((o0, o1, o2, o3)):
            at = pl.multiple_of((scal[1] ^ x) * rows, rows)
            ref[...] = wide[:, pl.ds(at, rows)].T.astype(BF16)


def attend_call(scal, seg_row, seg_col, q, k, vt, rows):
    length, wide = q.shape
    heads = wide // LANES
    width = heads * HD
    row = pl.BlockSpec((length, LANES), lambda h, s: (0, h))
    out = whole((rows, width))
    out_t = jax.ShapeDtypeStruct((rows, width), BF16)
    return pl.pallas_call(
        functools.partial(attend_kernel, 512),
        grid_spec=pltpu.PrefetchScalarGridSpec(
            num_scalar_prefetch=1,
            grid=(heads,),
            in_specs=[
                whole((1, length)), whole((length, 1)), row, row,
                pl.BlockSpec((LANES, length), lambda h, s: (h, 0)),
            ],
            out_specs=[
                pl.BlockSpec((HD, length), lambda h, s: (h, 0)),
                pl.BlockSpec((1, 1, length), lambda h, s: (h, 0, 0)),
                out, out, out, out,
            ],
            scratch_shapes=[pltpu.VMEM((width, length), F32)],
        ),
        out_shape=[
            jax.ShapeDtypeStruct((width, length), BF16),
            jax.ShapeDtypeStruct((heads, 1, length), F32),
            out_t, out_t, out_t, out_t,
        ],
        compiler_params=params(),
        cost_estimate=cost(heads * 4 * length * length * LANES, 8 * length * wide),
        name="attend",
    )(scal, seg_row, seg_col, q, k, vt)


def attend_back_kernel(
    step, scal, seg_row, seg_col, q_ref, k_ref, v_ref, kt_ref, ot_ref, lse_ref,
    d0, d1, d2, d3, dq_ref, dk_ref, dv_ref, grad_t, dk_sum, dv_sum,
):
    h = pl.program_id(0)
    length = q_ref.shape[0]

    @pl.when(h == 0)
    def _():
        rows = d0.shape[0]
        for x, ref in enumerate((d0, d1, d2, d3)):
            at = pl.multiple_of((scal[1] ^ x) * rows, rows)
            grad_t[:, pl.ds(at, rows)] = ref[...].astype(F32).T.astype(BF16)

    mine = grad_t[pl.ds(pl.multiple_of(h * HD, 16), HD), :]
    row_dot = jnp.sum(mine.astype(F32) * ot_ref[...].astype(F32), axis=0, keepdims=True)
    dv_sum[:, HD:] = jnp.zeros((length, LANES - HD), F32)
    for i in range(length // step):
        start, last = i * step, (i + 1) * step
        grad = mine[:, start:last]
        s = nt(k_ref[:last], q_ref[start:last])
        dp = nn(v_ref[:last, :HD], grad)
        s = jnp.where(allowed_mask(seg_row, seg_col, 0, last, start, step), s, NEG)
        p = jnp.exp2(s - lse_ref[0, :, start:last])
        ds = (p * (dp - row_dot[:, start:last])).astype(BF16)
        dv = nt(p.astype(BF16), grad)
        dk = nn(ds, q_ref[start:last])
        dqt = nn(kt_ref[:HD, :last], ds)
        if start:
            dv_sum[:start, :HD] += dv[:start]
            dk_sum[:start] += dk[:start]
        dv_sum[start:last, :HD] = dv[start:]
        dk_sum[start:last] = dk[start:]
        dq_ref[start:last, :HD] = (dqt * SCORE_SCALE).T.astype(BF16)
        dq_ref[start:last, HD:] = jnp.zeros((step, LANES - HD), BF16)
    dk_ref[...] = (dk_sum[...] * (1.0 / LOG2E)).astype(BF16)
    dv_ref[...] = dv_sum[...].astype(BF16)


def attend_back_call(scal, seg_row, seg_col, q, k, v, kt, ot, lse, grads):
    length, wide = q.shape
    heads = wide // LANES
    width = heads * HD
    rows = grads[0].shape[0]
    row = pl.BlockSpec((length, LANES), lambda h, s: (0, h))
    row_t = jax.ShapeDtypeStruct((length, wide), BF16)
    return pl.pallas_call(
        functools.partial(attend_back_kernel, 256),
        grid_spec=pltpu.PrefetchScalarGridSpec(
            num_scalar_prefetch=1,
            grid=(heads,),
            in_specs=[
                whole((1, length)), whole((length, 1)), row, row, row,
                pl.BlockSpec((LANES, length), lambda h, s: (h, 0)),
                pl.BlockSpec((HD, length), lambda h, s: (h, 0)),
                pl.BlockSpec((1, 1, length), lambda h, s: (h, 0, 0)),
            ]
            + [whole((rows, width))] * 4,
            out_specs=[row, row, row],
            scratch_shapes=[
                pltpu.VMEM((width, length), BF16),
                pltpu.VMEM((length, LANES), F32),
                pltpu.VMEM((length, LANES), F32),
            ],
        ),
        out_shape=[row_t, row_t, row_t],
        compiler_params=params(),
        cost_estimate=cost(heads * 8 * length * length * LANES, 16 * length * wide),
        name="attend_back",
    )(scal, seg_row, seg_col, q, k, v, kt, ot, lse, *grads)


def middle_kernel(
    scal, x_ref, g_ref, a0, a1, a2, a3, s0, s1, s2, s3, w0, w1, w2, w3,
    orr, ulr, drr,
    act_ref, gm_ref, o0, o1, o2, o3, e0, e1, e2, e3,
    wo, wu, wd, ol, ur, dl, sems, e_sum,
):
    c = pl.program_id(0)
    width = a0.shape[1]
    rank = orr.shape[1]
    copies = []
    for n, dst in enumerate((wo, wu, wd)):
        for x, src in enumerate((w0, w1, w2, w3)):
            copies.append(
                pltpu.make_async_copy(
                    src.at[pl.ds(n * width, width)],
                    dst.at[pl.ds(x * width, width)],
                    sems.at[n * 4 + x],
                )
            )

    @pl.when(c == 0)
    def _():
        for copy in copies:
            copy.start()
        for x, src in enumerate((s0, s1, s2, s3)):
            for slot, dst in enumerate((ol, ur, dl)):
                dst[:, x * width : (x + 1) * width] = src[:, slot * SLOT : slot * SLOT + width].astype(F32)
        e_sum[...] = jnp.zeros_like(e_sum)
        for copy in copies:
            copy.wait()

    out_lower, up_raise, down_lower = (r[...].astype(BF16) for r in (ol, ur, dl))
    out_raise, up_lower, down_raise = orr[0], ulr[0], drr[0]
    att = jnp.concatenate([a[...].astype(F32) for a in (a0, a1, a2, a3)], axis=1).astype(BF16)
    low_out = nt(att, out_lower).astype(BF16)
    middle = x_ref[...].astype(F32) + nn(att, wo[...]) + nn(low_out, out_raise)
    factor = lax.rsqrt(jnp.mean(middle * middle, axis=-1, keepdims=True) + EPS)
    unit = middle * factor
    normed = unit.astype(BF16)
    low_up = nt(normed, up_lower).astype(BF16)
    preact = nt(normed, wu[...]) + nn(low_up, up_raise)
    sigma = 1.0 / (1.0 + jnp.exp(-preact))
    active = (preact * sigma).astype(BF16)
    low_down = nt(active, down_lower).astype(BF16)
    act_ref[...] = (middle + (nn(active, wd[...]) + nn(low_down, down_raise))).astype(BF16)

    grad = g_ref[...]
    grad_low_down = nt(grad, down_raise).astype(BF16)
    grad_act = nt(grad, wd[...]) + nn(grad_low_down, down_lower)
    grad_pre = (grad_act * (sigma * (1.0 + preact * (1.0 - sigma)))).astype(BF16)
    grad_low_up = nt(grad_pre, up_raise).astype(BF16)
    grad_mid = nn(grad_pre, wu[...]) + nn(grad_low_up, up_lower)
    dot = jnp.mean(grad_mid * unit, axis=-1, keepdims=True)
    grad_middle = grad.astype(F32) + factor * (grad_mid - unit * dot)
    gm_ref[...] = grad_middle
    grad_attn = grad_middle.astype(BF16)
    grad_low_out = nt(grad_attn, out_raise).astype(BF16)
    grad_att = nt(grad_attn, wo[...]) + nn(grad_low_out, out_lower)
    for x, ref in enumerate((o0, o1, o2, o3)):
        ref[...] = grad_att[:, x * width : (x + 1) * width].astype(BF16)

    e_sum[0:rank] += tn(low_out, grad_attn)
    e_sum[rank : 2 * rank] += tn(grad_low_up, normed)
    e_sum[2 * rank : 3 * rank] += tn(low_down, grad)
    e_sum[3 * rank : 4 * rank] += tn(grad_low_out, att)
    e_sum[4 * rank : 5 * rank] += tn(low_up, grad_pre)
    e_sum[5 * rank : 6 * rank] += tn(grad_low_down, active)

    @pl.when(c == pl.num_programs(0) - 1)
    def _():
        shared = e_sum[: 3 * rank].astype(BF16)
        for x, ref in enumerate((e0, e1, e2, e3)):
            ref[: 3 * rank] = shared
            mark = jnp.full((rank, ref.shape[1]), scal[0], jnp.int32).astype(F32)
            if x:
                mark = jnp.zeros_like(mark)
            ref[3 * rank :] = mark.astype(BF16)
            for slot in range(3):
                part = e_sum[(3 + slot) * rank : (4 + slot) * rank, x * width : (x + 1) * width]
                ref[3 * rank :, slot * SLOT : slot * SLOT + width] = part.astype(BF16)


def middle_call(scal, x, g, att, pieces, weights, out_raise, up_lower, down_raise):
    rows, depth = x.shape
    width = att[0].shape[1]
    rank = out_raise.shape[1]
    step = 256
    wide = pl.BlockSpec((step, depth), lambda c, s: (c, 0))
    part = pl.BlockSpec((step, width), lambda c, s: (c, 0))
    small = pl.BlockSpec((rank, depth), lambda c, s: (rows // rank, 0))
    pick = pl.BlockSpec((1, rank, depth), lambda c, s: (s[0], 0, 0))
    any_spec = pl.BlockSpec(memory_space=pl.ANY)
    part_t = jax.ShapeDtypeStruct((rows, width), BF16)
    pack_t = jax.ShapeDtypeStruct((4 * rank, depth), BF16)
    square = pltpu.VMEM((4 * width, depth), BF16)
    thin = pltpu.VMEM((rank, depth), F32)
    return pl.pallas_call(
        middle_kernel,
        grid_spec=pltpu.PrefetchScalarGridSpec(
            num_scalar_prefetch=1,
            grid=(rows // step,),
            in_specs=[wide, wide] + [part] * 4 + [small] * 4 + [any_spec] * 4 + [pick] * 3,
            out_specs=[wide, wide] + [part] * 4 + [whole((4 * rank, depth))] * 4,
            scratch_shapes=[
                square, square, square, thin, thin, thin,
                pltpu.SemaphoreType.DMA((12,)),
                pltpu.VMEM((6 * rank, depth), F32),
            ],
        ),
        out_shape=[
            jax.ShapeDtypeStruct((rows, depth), BF16),
            jax.ShapeDtypeStruct((rows, depth), F32),
        ]
        + [part_t] * 4
        + [pack_t] * 4,
        compiler_params=params(),
        cost_estimate=cost(12 * rows * depth * depth, 6 * depth * depth + 12 * rows * depth),
        name="feed_forward",
    )(scal, x, g, *att, *pieces, *weights, out_raise, up_lower, down_raise)


def grad_in_kernel(
    heads, scal, dq, dk, dv, low, p0, p1, p2, p3, wq, wk, wv, lq, lk, lv, rq, rk, rv,
    out_ref, pack_ref, buf, sems, lower_sum, raise_sum,
):
    x = pl.program_id(0)
    rows = buf.shape[1]
    rank = lq.shape[1]
    pieces = (p0, p1, p2, p3)
    copies = [
        pltpu.make_async_copy(pieces[n].at[pl.ds(0, rows)], buf.at[n], sems.at[n])
        for n in range(4)
    ]

    @pl.when(x == 0)
    def _():
        for c in copies:
            c.start()
        lower_sum[...] = jnp.zeros_like(lower_sum)
        raise_sum[...] = jnp.zeros_like(raise_sum)

    for n in range(4):

        @pl.when(x == n)
        def _(n=n):
            copies[n].wait()

    block = buf[x]
    total = None
    low_grads = []
    for n, (d, w, r) in enumerate(((dq, wq, rq), (dk, wk, rk), (dv, wv, rv))):
        value = d[...]
        raise_pad = pad_heads(r[0].astype(F32), heads).astype(BF16)
        low_grads.append(nt(value, raise_pad))
        term = nt(value, w[...])
        total = term if total is None else total + term
        raise_sum[n * rank : (n + 1) * rank] += tn(low[:, n * rank : (n + 1) * rank], value)
    grad_low = jnp.concatenate(low_grads, axis=1).astype(BF16)
    lower = jnp.concatenate([lq[0], lk[0], lv[0]], axis=0)
    out_ref[0] = (total + nn(grad_low, lower)).astype(BF16)
    lower_sum[...] += tn(grad_low, block)

    @pl.when(x == pl.num_programs(0) - 1)
    def _():
        pack_ref[: 3 * rank] = lower_sum[...].astype(BF16)
        pack_ref[3 * rank :] = jnp.zeros((rank, pack_ref.shape[1]), BF16)
        for n in range(3):
            for h in range(heads):
                part = raise_sum[n * rank : (n + 1) * rank, h * LANES : h * LANES + HD]
                at = n * SLOT + h * HD
                pack_ref[3 * rank :, at : at + HD] = part.astype(BF16)


def grad_in_call(scal, grads, low, pieces, padded, lowers, raises, rows):
    depth, wide = padded[0].shape
    heads = wide // LANES
    rank = lowers[0].shape[1]
    width = raises[0].shape[2]
    any_spec = pl.BlockSpec(memory_space=pl.ANY)
    lower = pl.BlockSpec((1, rank, depth), lambda g, s: (s[0], 0, 0))
    raise_ = pl.BlockSpec((1, rank, width), lambda g, s: (s[0], 0, 0))
    row = pl.BlockSpec((rows, wide), lambda g, s: (s[1] ^ g, 0))
    low_spec = pl.BlockSpec((rows, 3 * rank), lambda g, s: (s[1] ^ g, 0))
    return pl.pallas_call(
        functools.partial(grad_in_kernel, heads),
        grid_spec=pltpu.PrefetchScalarGridSpec(
            num_scalar_prefetch=1,
            grid=(4,),
            in_specs=[row] * 3 + [low_spec] + [any_spec] * 4 + [whole((depth, wide))] * 3
            + [lower] * 3 + [raise_] * 3,
            out_specs=[
                pl.BlockSpec((1, rows, depth), lambda g, s: (g, 0, 0)),
                whole((4 * rank, depth)),
            ],
            scratch_shapes=[
                pltpu.VMEM((4, rows, depth), BF16),
                pltpu.SemaphoreType.DMA((4,)),
                pltpu.VMEM((3 * rank, depth), F32),
                pltpu.VMEM((3 * rank, wide), F32),
            ],
        ),
        out_shape=[
            jax.ShapeDtypeStruct((4, rows, depth), BF16),
            jax.ShapeDtypeStruct((4 * rank, depth), BF16),
        ],
        compiler_params=params(),
        cost_estimate=cost(8 * rows * depth * wide * 3, 16 * rows * depth),
        name="grad_input",
    )(scal, *grads, low, *pieces, *padded, *lowers, *raises)


def last_kernel(x_ref, gm_ref, a_ref, b_ref, c_ref, out_ref):
    x = x_ref[...].astype(F32)
    factor = lax.rsqrt(jnp.mean(x * x, axis=-1, keepdims=True) + EPS)
    unit = x * factor
    grad = a_ref[0].astype(F32) + b_ref[...].astype(F32) + c_ref[...].astype(F32)
    dot = jnp.mean(grad * unit, axis=-1, keepdims=True)
    out_ref[...] = (gm_ref[...] + factor * (grad - unit * dot)).astype(BF16)


def last_call(x, gm, a, b, c):
    rows, depth = x.shape
    step = 128
    wide = pl.BlockSpec((step, depth), lambda g: (g, 0))
    return pl.pallas_call(
        last_kernel,
        grid=(rows // step,),
        in_specs=[wide, wide, pl.BlockSpec((1, step, depth), lambda g: (0, g, 0)), wide, wide],
        out_specs=wide,
        out_shape=jax.ShapeDtypeStruct((rows, depth), BF16),
        compiler_params=params(),
        name="input_gradient",
    )(x, gm, a, b, c)


def sets_kernel(first_ref, second_ref, *outs):
    j = pl.program_id(0)
    rank = outs[0].shape[1]
    depth = first_ref.shape[2]
    sums = [jnp.zeros(first_ref.shape[1:], F32) for _ in range(2)]
    for n in range(first_ref.shape[0]):
        chosen = first_ref[n, 3 * rank : 3 * rank + 1, depth - 1 : depth].astype(F32)
        pick = (chosen == j.astype(F32)).astype(F32)
        for m, ref in enumerate((first_ref, second_ref)):
            sums[m] = sums[m] + ref[n].astype(F32) * pick
    for m, total in enumerate(sums):
        for k in range(3):
            outs[6 * m + k][0] = total[k * rank : (k + 1) * rank]
            width = outs[6 * m + 3 + k].shape[2]
            outs[6 * m + 3 + k][0] = total[3 * rank :, k * SLOT : k * SLOT + width]


def sets_call(first, second, sets, width):
    parts, four, depth = first.shape
    rank = four // 4
    full = pl.BlockSpec((1, rank, depth), lambda j: (j, 0, 0))
    thin = pl.BlockSpec((1, rank, width), lambda j: (j, 0, 0))
    full_t = jax.ShapeDtypeStruct((sets, rank, depth), F32)
    thin_t = jax.ShapeDtypeStruct((sets, rank, width), F32)
    return pl.pallas_call(
        sets_kernel,
        grid=(sets,),
        in_specs=[whole(first.shape), whole(second.shape)],
        out_specs=[full, full, full, thin, thin, thin] * 2,
        out_shape=[full_t, full_t, full_t, thin_t, thin_t, thin_t] * 2,
        compiler_params=params(),
        name="set_sums",
    )(first, second)


def on_device(
    dp_count,
    tensor_count,
    tokens,
    segment_ids,
    adapter_choice,
    cotangent,
    weight_query,
    weight_key,
    weight_value,
    weight_output,
    weight_upward,
    weight_downward,
    query_lower,
    query_raise,
    key_lower,
    key_raise,
    value_lower,
    value_raise,
    output_lower,
    output_raise,
    upward_lower,
    upward_raise,
    downward_lower,
    downward_raise,
):
    across = functools.partial(swap, axis_name="tensor", count=tensor_count)
    x, g = tokens[0], cotangent[0]
    rows = x.shape[0]
    length = segment_ids.shape[1]
    sets, rank = query_lower.shape[:2]
    me = lax.axis_index("tensor").astype(jnp.int32)
    scal = jnp.stack([adapter_choice[0], me])
    seg_row = segment_ids
    seg_col = segment_ids.reshape(length, 1)

    own = norm_call(x, adapter_choice, output_lower, upward_raise, downward_lower)
    far = across(own, bit=2)
    near = across(own, bit=1)
    pq, pk, pv, wt = prep_call(
        weight_query, weight_key, weight_value, weight_output, weight_upward, weight_downward
    )
    share = wt.shape[0] // dp_count
    mine = lax.dynamic_slice_in_dim(wt, lax.axis_index("dp") * share, share, 0)
    fetched = across(mine, bit=2)
    wt_far = lax.all_gather(fetched, "dp", axis=0, tiled=True)
    wt_near = across(wt, bit=1)
    wt_cross = across(wt_far, bit=1)

    cross = across(far, bit=1)
    pieces = (own, near, far, cross)
    lowers = (query_lower, key_lower, value_lower)
    raises = (query_raise, key_raise, value_raise)
    padded = (pq, pk, pv)
    q, k, v, kt, vt, low = qkv_call(scal, pieces, padded, lowers, raises, rows, length)
    ot, lse, *att = attend_call(scal, seg_row, seg_col, q, k, vt, rows)
    att = [att[0]] + [across(att[n], bit=n) for n in (1, 2, 3)]
    act, grad_middle, *more = middle_call(
        scal, x, g, att, pieces, (wt, wt_near, wt_far, wt_cross),
        output_raise, upward_lower, downward_raise,
    )
    grads, packs = more[:4], more[4:]
    grads = [grads[0]] + [across(grads[n], bit=n) for n in (1, 2, 3)]
    packs = [packs[0]] + [across(packs[n], bit=n) for n in (1, 2, 3)]
    packs = [p.astype(F32) for p in packs]
    first = ((packs[0] + packs[1]) + (packs[2] + packs[3])).astype(BF16)
    first_all = lax.all_gather(first, "dp", axis=0)

    back = attend_back_call(scal, seg_row, seg_col, q, k, v, kt, ot, lse, grads)
    partial, pack = grad_in_call(scal, back, low, pieces, padded, lowers, raises, rows)

    lower_part = pack[: 3 * rank]
    others = [across(lower_part, bit=n).astype(F32) for n in (1, 2, 3)]
    lower_sum = (lower_part.astype(F32) + others[0]) + (others[1] + others[2])
    second = jnp.concatenate([lower_sum.astype(BF16), pack[3 * rank :]], axis=0)
    second_all = lax.all_gather(second, "dp", axis=0)

    near_mine = across(partial[1], bit=1)
    near_far = across(partial[3], bit=1)
    to_far = (partial[2].astype(F32) + near_far.astype(F32)).astype(BF16)
    from_far = across(to_far, bit=2)
    input_grad = last_call(x, grad_middle, partial, near_mine, from_far)

    out = sets_call(first_all, second_all, sets, query_raise.shape[2])
    (out_raise_g, up_lower_g, down_raise_g, out_lower_g, up_raise_g, down_lower_g) = out[:6]
    (q_lower_g, k_lower_g, v_lower_g, q_raise_g, k_raise_g, v_raise_g) = out[6:]
    return (
        act[None],
        input_grad[None],
        q_lower_g,
        q_raise_g,
        k_lower_g,
        k_raise_g,
        v_lower_g,
        v_raise_g,
        out_lower_g,
        out_raise_g,
        up_lower_g,
        up_raise_g,
        down_lower_g,
        down_raise_g,
    )


def solution(mesh):
    split = P(None, None, "tensor")
    return jax.shard_map(
        functools.partial(on_device, mesh.shape["dp"], mesh.shape["tensor"]),
        mesh=mesh,
        in_specs=(
            P("dp", "tensor", None),
            P("dp", None),
            P("dp"),
            P("dp", "tensor", None),
            P(None, "tensor"),
            P(None, "tensor"),
            P(None, "tensor"),
            P(None, "tensor"),
            P(None, "tensor"),
            P(None, "tensor"),
            P(),
            split,
            P(),
            split,
            P(),
            split,
            split,
            P(),
            P(),
            split,
            split,
            P(),
        ),
        out_specs=(
            P("dp", "tensor", None),
            P("dp", "tensor", None),
            P(),
            split,
            P(),
            split,
            P(),
            split,
            split,
            P(),
            P(),
            split,
            split,
            P(),
        ),
        check_vma=False,
    )
```

time: 1210 us -> 338 us (0.28)
  blocking collectives: 391 us -> 0 us
  matrix products: 306 us -> 0 us
  waiting for transfers between devices: 308 us -> 135 us
  Pallas kernels: 0 us -> 149 us
  other arithmetic: 109 us -> 6.07 us
  local copies, waits for them, and re-layouts: 53.7 us -> 16.4 us
  starting transfers between devices: 1.13 us -> 17.3 us
  loops' own time: 13.6 us -> 0 us
    all_gather x12 -> x0, blocking collectives: 369 us -> none  [the longest x1 31.2 us: on_device(): lax.all_gather(summed_out_raise[None].astype(jnp.bfloat16), 'dp', axis=0,...]
    dot_general x94 -> x0, matrix products: 306 us -> none  [the longest x4 59.6 us: backward_block(): jnp.einsum('qhd,khd->hqk', grad_piece, values_all, preferred_element_type...]
    reduce_scatter x4 -> x0, waiting for transfers between devices: 170 us -> none  [the longest x1 85.4 us: on_device(): lax.psum_scatter(grad_mid_terms, 'tensor', scatter_dimension=0, tiled=True)]
    pallas_call x0 -> x9, Pallas kernels: none -> 149 us  [the longest x1 30.9 us: attend_back_call(): pl.pallas_call(functools.partial(attend_back_kernel, 256), grid_spec=pltp...]
    all_gather x4 -> x3, waiting for transfers between devices: 137 us -> 55.2 us  [the longest x1 35.8 us: on_device(): second_all = lax.all_gather(second, 'dp', axis=0)]
    ppermute x0 -> x21, waiting for transfers between devices: none -> 79.5 us  [swap(): return lax.ppermute(array, axis_name, [(i, i ^ bit) for i in range(count)])]
    convert_element_type x10 -> x3, other arithmetic: 62.5 us -> 4.81 us  [the longest x1 3.07 us: on_device(): to_far = (partial[2].astype(F32) + near_far.astype(F32)).astype(BF16)]
    reduce_sum x8 -> x0, other arithmetic: 27.7 us -> none  [the longest x4 17.9 us: forward_block(): row_total = jnp.sum(exponent, axis=-1, keepdims=True)]
  transfers between devices with their start and end apart: 10 -> 24, of which waited for: 6 -> 13; matrix products, arithmetic and copies ran while one was open for 6% -> 3% of each run, Pallas kernels for 0% -> 31%
where the time goes in v1:
time: 338 us
  Pallas kernels  149 us (44%)
  waiting for transfers between devices  135 us (40%)
  starting transfers between devices  17.3 us (5%)
  local copies, waits for them, and re-layouts  16.4 us (5%)
  between operations  14.6 us (4%)
  other arithmetic  6.07 us (2%)
    ppermute x21, waiting for transfers between devices, swap(): return lax.ppermute(array, axis_name, [(i, i ^ bit) for i in range(count)])  79.5 us
    all_gather x1, waiting for transfers between devices, on_device(): second_all = lax.all_gather(second, 'dp', axis=0)  35.8 us
    pallas_call x1, Pallas kernels, attend_back_call(): pl.pallas_call(functools.partial(attend_back_kernel, 256), grid_spec=pltp...  30.9 us
    pallas_call x1, Pallas kernels, middle_call(): pl.pallas_call(middle_kernel, grid_spec=pltpu.PrefetchScalarGridSpec(num_...  30.6 us
    pallas_call x1, Pallas kernels, attend_call(): pl.pallas_call(functools.partial(attend_kernel, 512), grid_spec=pltpu.Pre...  20.7 us
    pallas_call x1, Pallas kernels, qkv_call(): pl.pallas_call(functools.partial(qkv_kernel, heads), grid_spec=pltpu.Pref...  20.6 us
    pallas_call x1, Pallas kernels, grad_in_call(): pl.pallas_call(functools.partial(grad_in_kernel, heads), grid_spec=pltpu....  20 us
    all_gather x1, waiting for transfers between devices, on_device(): wt_far = lax.all_gather(fetched, 'dp', axis=0, tiled=True)  19.4 us
  transfers between devices with their start and end apart: 24, of which 13 were waited for; matrix products, arithmetic and copies ran while one was open for 3% of the time, Pallas kernels for 31%

profile of v1, /device:TPU:0, one launch (start us, length us, event | category | flops | bytes accessed | tf_op | source)
XLA Modules:
  0.0 337.7 jit_solution(11981923981733867419)
XLA Ops:
  7.2 0.0 all-gather.6.cloned.1.call-start
  7.2 2.3 copy.42.wq
  9.5 1.3 copy.43.wk
  10.8 1.3 copy.44.wv
  12.1 1.3 copy.45.wo
  13.4 1.3 copy.46.wu
  14.7 1.3 copy.47.wd
  16.0 8.0 %weight_layouts.1 = (bf16[1280,512]{1,0:T(8,128)(2,1)}, bf16[1280,512]{1,0:T(8,128)(2,1)}, bf16[1280,512]{1,0:T(8,128)(2,1)}, bf16[960,1280]{1,0:T(8,128)(2,1)}) custom-call(bf16[1280,320]{1,0:T(8,128)(2,1)} %copy.42.wq, bf16[1280,320]{1,0:T(8,128)(2,1)} %copy.43.wk, bf16[1280,320]{1,0:T(8,128)(2,1)} %copy.44.wv, bf16[1280,320]{1,0:T(8,128)(2,1)} %copy.45.wo, ...), custom_call_target="tpu_custom_call" | custom-call | tf_op jit(solution)/shard_map/weight_layouts/pallas_call | solution.py:104
  24.0 1.0 constant_dynamic-slice_fusion
  25.0 3.0 collective-permute-start.7
  28.0 7.3 %collective-permute-done.7 = bf16[120,1280]{1,0:T(8,128)(2,1)S(1)} collective-permute-done((bf16[120,1280]{1,0:T(8,128)(2,1)S(1)}, bf16[120,1280]{1,0:T(8,128)(2,1)S(1)}, u32[]{:S(2)}, u32[]{:S(2)}) %collective-permute-start.7) | collective-permute-done | bytes 307232 | tf_op jit(solution)/shard_map/ppermute | solution.py:51
  35.3 0.7 copy-done.7
  36.0 0.0 all-gather.6.cloned.1.call-update
  36.0 0.0 all-gather.8.cloned.1.call-start
  36.7 0.0 copy-start.9
  36.8 3.0 norm_in.1.p0.s0
  39.8 1.7 collective-permute-start.1
  41.5 29.4 %collective-permute-done.1.p2.s2 = bf16[528,1280]{1,0:T(8,128)(2,1)} collective-permute-done((bf16[528,1280]{1,0:T(8,128)(2,1)}, bf16[528,1280]{1,0:T(8,128)(2,1)}, u32[]{:S(2)}, u32[]{:S(2)}) %collective-permute-start.1) | collective-permute-done | bytes 1351712 | tf_op jit(solution)/shard_map/ppermute | solution.py:51
  70.9 0.0 collective-permute-start.2
  70.9 0.5 collective-permute-start.6
  71.4 19.4 %all-gather.6.cloned.1.call-done.w2 = bf16[960,1280]{1,0:T(8,128)(2,1)} async-done(((bf16[120,1280]{1,0:T(8,128)(2,1)}), bf16[960,1280]{1,0:T(8,128)(2,1)}) %all-gather.6.cloned.1.call-update) | async-done | bytes 2457616 | tf_op jit(solution)/shard_map/all_gather | solution.py:654
  90.8 1.4 copy.48.seg_col
  92.2 0.6 pad_add_fusion.scal
  92.8 20.6 %project.1 = (bf16[2048,512]{1,0:T(8,128)(2,1)}, bf16[2048,512]{1,0:T(8,128)(2,1)}, bf16[2048,512]{1,0:T(8,128)(2,1)}, bf16[512,2048]{1,0:T(8,128)(2,1)}, bf16[5...) custom-call(s32[2]{0:T(128)} %pad_add_fusion.scal, bf16[528,1280]{1,0:T(8,128)(2,1)} %norm_in.1.p0.s0, ...), custom_call_target="tpu_custom_call" | custom-call | flops 8053063680 | bytes 12582912 | tf_op jit(solution)/shard_map/project/pallas_call | solution.py:176
  113.3 20.7 %attend.1 = (bf16[320,2048]{1,0:T(8,128)(2,1)}, f32[4,1,2048]{2,1,0:T(1,128)}, bf16[512,320]{1,0:T(8,128)(2,1)}, bf16[512,320]{1,0:T(8,128)(2,1)}, bf16[512,320]{1,0:T(8,128)(2,1)}, /*index=5*/bf16[512,320]{1,0:T(8,128)(2,1)}) custom-call(s32[2]{0:T(128)} %pad_add_fusion.scal, s32[1,2048]{1,0:T(1,128)} %seg_row.3, s32[2048,1]{1,0:T(8,128)} %copy.48.seg_col, ...), custom_call_target="tpu_custom_call" | custom-call | flops 8589934592 | bytes 8388608 | tf_op jit(solution)/shard_map/attend/pallas_call | solution.py:240
  134.0 0.5 collective-permute-start.3
  134.6 1.5 collective-permute-start.4
  136.1 0.1 collective-permute-done.3.a1
  136.2 10.6 %collective-permute-done.4.a2 = bf16[512,320]{1,0:T(8,128)(2,1)S(1)} collective-permute-done((bf16[512,320]{1,0:T(8,128)(2,1)}, bf16[512,320]{1,0:T(8,128)(2,1)S(1)}, u32[]{:S(2)}, u32[]{:S(2)}) %collective-permute-start.4) | collective-permute-done | bytes 327712 | tf_op jit(solution)/shard_map/ppermute | solution.py:51
  146.8 6.7 %collective-permute-done.5.a3 = bf16[512,320]{1,0:T(8,128)(2,1)S(1)} collective-permute-done((bf16[512,320]{1,0:T(8,128)(2,1)}, bf16[512,320]{1,0:T(8,128)(2,1)S(1)}, u32[]{:S(2)}, u32[]{:S(2)}) %collective-permute-start.5) | collective-permute-done | bytes 327712 | tf_op jit(solution)/shard_map/ppermute | solution.py:51
  153.5 0.7 copy-done.15
  154.2 30.6 %feed_forward.1 = (bf16[512,1280]{1,0:T(8,128)(2,1)}, f32[512,1280]{1,0:T(8,128)}, bf16[512,320]{1,0:T(8,128)(2,1)}, bf16[512,320]{1,0:T(8,128)(2,1)}, bf16[512,...) custom-call(s32[2]{0:T(128)} %pad_add_fusion.scal, ...), custom_call_target="tpu_custom_call" | custom-call | flops 10066329600 | bytes 17694720 | tf_op jit(solution)/shard_map/feed_forward/pallas_call | solution.py:435
  184.8 0.8 collective-permute-start.15
  185.5 1.5 collective-permute-start.16
  187.0 0.7 collective-permute-start.9
  187.7 1.5 collective-permute-start.10
  189.2 3.6 %collective-permute-done.16 = bf16[64,1280]{1,0:T(8,128)(2,1)S(1)} collective-permute-done((bf16[64,1280]{1,0:T(8,128)(2,1)}, bf16[64,1280]{1,0:T(8,128)(2,1)S(1)}, u32[]{:S(2)}, u32[]{:S(2)}) %collective-permute-start.16) | collective-permute-done | bytes 163872 | tf_op jit(solution)/shard_map/ppermute | solution.py:51
  192.8 2.6 collective-permute-done.17
  195.4 1.7 add_convert_fusion
  197.1 0.0 all-gather.8.cloned.1.call-update
  197.1 0.0 all-gather.10.cloned.1.call-start
  197.2 0.0 copy-start.10
  197.2 7.6 %collective-permute-done.10.d2 = bf16[512,320]{1,0:T(8,128)(2,1)S(1)} collective-permute-done((bf16[512,320]{1,0:T(8,128)(2,1)}, bf16[512,320]{1,0:T(8,128)(2,1)S(1)}, u32[]{:S(2)}, u32[]{:S(2)}) %collective-permute-start.10) | collective-permute-done | bytes 327712 | tf_op jit(solution)/shard_map/ppermute | solution.py:51
  204.7 6.7 %collective-permute-done.11.d3 = bf16[512,320]{1,0:T(8,128)(2,1)S(1)} collective-permute-done((bf16[512,320]{1,0:T(8,128)(2,1)}, bf16[512,320]{1,0:T(8,128)(2,1)S(1)}, u32[]{:S(2)}, u32[]{:S(2)}) %collective-permute-start.11) | collective-permute-done | bytes 327712 | tf_op jit(solution)/shard_map/ppermute | solution.py:51
  211.4 0.7 copy-done.12
  212.2 30.9 %attend_back.1 = (bf16[2048,512]{1,0:T(8,128)(2,1)}, bf16[2048,512]{1,0:T(8,128)(2,1)}, bf16[2048,512]{1,0:T(8,128)(2,1)}) custom-call(s32[2]{0:T(128)} %pad_add_fusion.scal, s32[1,2048]{1,0:T(1,128)} %seg_row.3, s32[2048,1]{1,0:T(8,128)} %copy.48.seg_col, bf16[2048,512]{1,0:T(8,128)(2,1)} %get-tuple-element.60.q_ref, ...), custom_call_target="tpu_custom_call" | custom-call | flops 17179869184 | bytes 16777216 | tf_op jit(solution)/shard_map/attend_back/pallas_call | solution.py:313
  243.0 20.0 %grad_input.1 = (bf16[4,512,1280]{2,1,0:T(8,128)(2,1)}, bf16[64,1280]{1,0:T(8,128)(2,1)}) custom-call(s32[2]{0:T(128)} %pad_add_fusion.scal, bf16[2048,512]{1,0:T(8,128)(2,1)} %get-tuple-element.78.dq, bf16[2048,512]{1,0:T(8,128)(2,1)} %get-tuple-element.79.dk, bf16[2048,512]{1,0:T(8,128)(2,1)} %get-tuple-element.80.dv, ...), custom_call_target="tpu_custom_call" | custom-call | flops 8053063680 | bytes 10485760 | tf_op jit(solution)/shard_map/grad_input/pallas_call | solution.py:522
  263.0 0.0 copy-start.6
  263.0 1.9 slice_bitcast_fusion
  264.9 1.2 collective-permute-start.13
  266.1 1.5 collective-permute-start.19
  267.6 0.7 collective-permute-start.20
  268.3 3.9 %collective-permute-done.19 = bf16[48,1280]{1,0:T(8,128)(2,1)S(1)} collective-permute-done((bf16[48,1280]{1,0:T(8,128)(2,1)S(1)}, bf16[48,1280]{1,0:T(8,128)(2,1)S(1)}, u32[]{:S(2)}, u32[]{:S(2)}) %collective-permute-start.19) | collective-permute-done | bytes 122912 | tf_op jit(solution)/shard_map/ppermute | solution.py:51
  272.3 1.0 collective-permute-done.20
  273.2 0.1 add_convert_fusion.1
  273.3 0.7 pad_maximum_fusion
  274.0 0.0 all-gather.10.cloned.1.call-update
  274.0 0.7 collective-permute-start.12
  274.7 3.1 fusion
  277.8 1.5 collective-permute-start.14
  279.3 35.8 %all-gather.10.cloned.1.call-done = bf16[512,1280]{1,0:T(8,128)(2,1)} async-done(((bf16[64,1280]{1,0:T(8,128)(2,1)}), bf16[512,1280]{1,0:T(8,128)(2,1)}) %all-gather.10.cloned.1.call-update) | async-done | bytes 1310736 | tf_op jit(solution)/shard_map/all_gather | solution.py:684
  315.1 9.7 %set_sums.1 = (f32[8,16,1280]{2,1,0:T(8,128)}, f32[8,16,1280]{2,1,0:T(8,128)}, f32[8,16,1280]{2,1,0:T(8,128)}, f32[8,16,320]{2,1,0:T(8,128)}, f32[8,16,320]{2,1,...) custom-call(bf16[8,64,1280]{2,1,0:T(8,128)(2,1)} %bitcast.19, ...), custom_call_target="tpu_custom_call" | custom-call | tf_op jit(solution)/shard_map/set_sums/pallas_call | solution.py:598
  324.8 1.1 copy-done
  325.9 5.3 %input_gradient.1 = bf16[512,1280]{1,0:T(8,128)(2,1)} custom-call(bf16[512,1280]{1,0:T(8,128)(2,1)} %bitcast.17, f32[512,1280]{1,0:T(8,128)} %get-tuple-element.69.gm_ref, bf16[4,512,1280]{2,1,0:T(8,128)(2,1)} %get-tuple-element.82.a_ref, bf16[512,1280]{1,0:T(8,128)(2,1)} %collective-permute-done.12.b_ref, bf16[512,1280]{1,0:T(8,128)(2,1)} %copy-done), custom_call_target="tpu_custom_call" | custom-call | tf_op jit(solution)/shard_map/input_gradient/pallas_call | solution.py:563
  (44 shorter events, 0.1 us)
Async XLA Ops:
  7.2 2.3 copy-start.1
  7.2 83.6 %all-gather.6.cloned.1.call-start = ((), (), s32[]{:S(2)}) async-start(), calls=%async_computation | async-start | bytes 2764800 | tf_op jit(solution)/shard_map/all_gather | solution.py:654
  9.5 1.3 copy-start.2
  10.8 1.3 copy-start.3
  12.1 1.3 copy-start.4
  13.4 1.3 copy-start.5
  25.0 10.3 %collective-permute-start.7 = (bf16[120,1280]{1,0:T(8,128)(2,1)S(1)}, bf16[120,1280]{1,0:T(8,128)(2,1)S(1)}, u32[]{:S(2)}, u32[]{:S(2)}) collective-permute-start(bf16[120,1280]{1,0:T(8,128)(2,1)S(1)} %constant_dynamic-slice_fusion), channel_id=1, source_target_pairs={{0,2},{1,3},{2,0},{3,1},{4,6},{5,7},{6,4},{7,5},{8,10},{9,11},{10,... | collective-permute-start | bytes 921608 | tf_op jit(solution)/shard_map/ppermute | solution.py:51
  35.3 0.7 copy-start.7
  36.0 243.2 %all-gather.8.cloned.1.call-start = ((), (), s32[]{:S(2)}) async-start(), calls=%async_computation.1 | async-start | bytes 1474560 | tf_op jit(solution)/shard_map/all_gather | solution.py:675
  36.7 34.2 %copy-start.8 = (bf16[960,1280]{1,0:T(8,128)(2,1)S(1)}, bf16[960,1280]{1,0:T(8,128)(2,1)}, u32[]{:S(2)}) copy-start(bf16[960,1280]{1,0:T(8,128)(2,1)} %get-tuple-element.67.w0) | copy-start | bytes 7372804
  36.7 54.1 %copy-start.9 = (s32[1,2048]{1,0:T(1,128)S(1)}, s32[1,2048]{1,0:T(1,128)}, u32[]{:S(2)}) copy-start(s32[1,2048]{1,0:T(1,128)} %seg_row.3) | copy-start | bytes 24580
  39.8 31.2 %collective-permute-start.1 = (bf16[528,1280]{1,0:T(8,128)(2,1)}, bf16[528,1280]{1,0:T(8,128)(2,1)}, u32[]{:S(2)}, u32[]{:S(2)}) collective-permute-start(bf16[528,1280]{1,0:T(8,128)(2,1)} %norm_in.1.p0.s0), channel_id=1, source_target_pairs={{0,2},{1,3},{2,0},{3,1},{4,6},{5,7},{6,4},{7,5},{8,10},{9,11},{10,... | collective-permute-start | bytes 4055048 | tf_op jit(solution)/shard_map/ppermute | solution.py:51
  41.5 51.3 %collective-permute-start = (bf16[528,1280]{1,0:T(8,128)(2,1)}, bf16[528,1280]{1,0:T(8,128)(2,1)}, u32[]{:S(2)}, u32[]{:S(2)}) collective-permute-start(bf16[528,1280]{1,0:T(8,128)(2,1)} %norm_in.1.p0.s0), channel_id=1, source_target_pairs={{0,1},{1,0},{2,3},{3,2},{4,5},{5,4},{6,7},{7,6},{8,9},{9,8},{10,11... | collective-permute-start | bytes 4055048 | tf_op jit(solution)/shard_map/ppermute | solution.py:51
  70.9 21.8 %collective-permute-start.2 = (bf16[528,1280]{1,0:T(8,128)(2,1)}, bf16[528,1280]{1,0:T(8,128)(2,1)}, u32[]{:S(2)}, u32[]{:S(2)}) collective-permute-start(bf16[528,1280]{1,0:T(8,128)(2,1)} %collective-permute-done.1.p2.s2), channel_id=1, source_target_pairs={{0,1},{1,0},{2,3},{3,2},{4,5},{5,4},{6,7},{7,6},{8,9},{9,8},{10,11... | collective-permute-start | bytes 4055048 | tf_op jit(solution)/shard_map/ppermute | solution.py:51
  70.9 65.1 %collective-permute-start.6 = (bf16[960,1280]{1,0:T(8,128)(2,1)S(1)}, bf16[960,1280]{1,0:T(8,128)(2,1)}, u32[]{:S(2)}, u32[]{:S(2)}) collective-permute-start(bf16[960,1280]{1,0:T(8,128)(2,1)S(1)} %copy-done.8), channel_id=1, source_target_pairs={{0,1},{1,0},{2,3},{3,2},{4,5},{5,4},{6,7},{7,6},{8,9},{9,8},{10,11... | collective-permute-start | bytes 7372808 | tf_op jit(solution)/shard_map/ppermute | solution.py:51
  90.8 62.7 %collective-permute-start.8 = (bf16[960,1280]{1,0:T(8,128)(2,1)}, bf16[960,1280]{1,0:T(8,128)(2,1)}, u32[]{:S(2)}, u32[]{:S(2)}) collective-permute-start(bf16[960,1280]{1,0:T(8,128)(2,1)} %all-gather.6.cloned.1.call-done.w2), channel_id=1, source_target_pairs={{0,1},{1,0},{2,3},{3,2},{4,5},{5,4},{6,7},{7,6},{8,9},{9,8},{10,11... | collective-permute-start | bytes 7372808 | tf_op jit(solution)/shard_map/ppermute | solution.py:51
  134.0 2.1 collective-permute-start.3
  134.6 12.2 %collective-permute-start.4 = (bf16[512,320]{1,0:T(8,128)(2,1)}, bf16[512,320]{1,0:T(8,128)(2,1)S(1)}, u32[]{:S(2)}, u32[]{:S(2)}) collective-permute-start(bf16[512,320]{1,0:T(8,128)(2,1)} %get-tuple-element.65), channel_id=1, source_target_pairs={{0,2},{1,3},{2,0},{3,1},{4,6},{5,7},{6,4},{7,5},{8,10},{9,11},{10,... | collective-permute-start | bytes 983048 | tf_op jit(solution)/shard_map/ppermute | solution.py:51
  136.1 17.4 %collective-permute-start.5 = (bf16[512,320]{1,0:T(8,128)(2,1)}, bf16[512,320]{1,0:T(8,128)(2,1)S(1)}, u32[]{:S(2)}, u32[]{:S(2)}) collective-permute-start(bf16[512,320]{1,0:T(8,128)(2,1)} %get-tuple-element.66), channel_id=1, source_target_pairs={{0,3},{1,2},{2,1},{3,0},{4,7},{5,6},{6,5},{7,4},{8,11},{9,10},{10,... | collective-permute-start | bytes 983048 | tf_op jit(solution)/shard_map/ppermute | solution.py:51
  136.2 17.3 %copy-start.13 = (bf16[512,320]{1,0:T(8,128)(2,1)}, bf16[512,320]{1,0:T(8,128)(2,1)S(1)}, u32[]{:S(2)}) copy-start(bf16[512,320]{1,0:T(8,128)(2,1)S(1)} %collective-permute-done.3.a1) | copy-start | bytes 983044
  146.8 6.7 %copy-start.14 = (bf16[512,320]{1,0:T(8,128)(2,1)}, bf16[512,320]{1,0:T(8,128)(2,1)S(1)}, u32[]{:S(2)}) copy-start(bf16[512,320]{1,0:T(8,128)(2,1)S(1)} %collective-permute-done.4.a2) | copy-start | bytes 983044
  153.4 0.7 copy-start.15
  184.8 4.4 %collective-permute-start.15 = (bf16[64,1280]{1,0:T(8,128)(2,1)}, bf16[64,1280]{1,0:T(8,128)(2,1)S(1)}, u32[]{:S(2)}, u32[]{:S(2)}) collective-permute-start(bf16[64,1280]{1,0:T(8,128)(2,1)} %get-tuple-element.84), channel_id=1, source_target_pairs={{0,1},{1,0},{2,3},{3,2},{4,5},{5,4},{6,7},{7,6},{8,9},{9,8},{10,11... | collective-permute-start | bytes 491528 | tf_op jit(solution)/shard_map/ppermute | solution.py:51
  185.5 7.3 %collective-permute-start.16 = (bf16[64,1280]{1,0:T(8,128)(2,1)}, bf16[64,1280]{1,0:T(8,128)(2,1)S(1)}, u32[]{:S(2)}, u32[]{:S(2)}) collective-permute-start(bf16[64,1280]{1,0:T(8,128)(2,1)} %get-tuple-element.85), channel_id=1, source_target_pairs={{0,2},{1,3},{2,0},{3,1},{4,6},{5,7},{6,4},{7,5},{8,10},{9,11},{10,... | collective-permute-start | bytes 491528 | tf_op jit(solution)/shard_map/ppermute | solution.py:51
  187.0 8.4 %collective-permute-start.17 = (bf16[64,1280]{1,0:T(8,128)(2,1)}, bf16[64,1280]{1,0:T(8,128)(2,1)S(1)}, u32[]{:S(2)}, u32[]{:S(2)}) collective-permute-start(bf16[64,1280]{1,0:T(8,128)(2,1)} %get-tuple-element.86), channel_id=1, source_target_pairs={{0,3},{1,2},{2,1},{3,0},{4,7},{5,6},{6,5},{7,4},{8,11},{9,10},{10,... | collective-permute-start | bytes 491528 | tf_op jit(solution)/shard_map/ppermute | solution.py:51
  187.0 10.2 %collective-permute-start.9 = (bf16[512,320]{1,0:T(8,128)(2,1)}, bf16[512,320]{1,0:T(8,128)(2,1)S(1)}, u32[]{:S(2)}, u32[]{:S(2)}) collective-permute-start(bf16[512,320]{1,0:T(8,128)(2,1)} %get-tuple-element.75), channel_id=1, source_target_pairs={{0,1},{1,0},{2,3},{3,2},{4,5},{5,4},{6,7},{7,6},{8,9},{9,8},{10,11... | collective-permute-start | bytes 983048 | tf_op jit(solution)/shard_map/ppermute | solution.py:51
  187.7 17.1 %collective-permute-start.10 = (bf16[512,320]{1,0:T(8,128)(2,1)}, bf16[512,320]{1,0:T(8,128)(2,1)S(1)}, u32[]{:S(2)}, u32[]{:S(2)}) collective-permute-start(bf16[512,320]{1,0:T(8,128)(2,1)} %get-tuple-element.76), channel_id=1, source_target_pairs={{0,2},{1,3},{2,0},{3,1},{4,6},{5,7},{6,4},{7,5},{8,10},{9,11},{10,... | collective-permute-start | bytes 983048 | tf_op jit(solution)/shard_map/ppermute | solution.py:51
  189.2 22.3 %collective-permute-start.11 = (bf16[512,320]{1,0:T(8,128)(2,1)}, bf16[512,320]{1,0:T(8,128)(2,1)S(1)}, u32[]{:S(2)}, u32[]{:S(2)}) collective-permute-start(bf16[512,320]{1,0:T(8,128)(2,1)} %get-tuple-element.77), channel_id=1, source_target_pairs={{0,3},{1,2},{2,1},{3,0},{4,7},{5,6},{6,5},{7,4},{8,11},{9,10},{10,... | collective-permute-start | bytes 983048 | tf_op jit(solution)/shard_map/ppermute | solution.py:51
  197.1 117.9 %all-gather.10.cloned.1.call-start = ((), (), s32[]{:S(2)}) async-start(), calls=%async_computation.2 | async-start | bytes 1474560 | tf_op jit(solution)/shard_map/all_gather | solution.py:684
  197.2 14.2 %copy-start.10 = (bf16[512,320]{1,0:T(8,128)(2,1)}, bf16[512,320]{1,0:T(8,128)(2,1)S(1)}, u32[]{:S(2)}) copy-start(bf16[512,320]{1,0:T(8,128)(2,1)S(1)} %collective-permute-done.9.d1) | copy-start | bytes 983044
  204.7 6.7 %copy-start.11 = (bf16[512,320]{1,0:T(8,128)(2,1)}, bf16[512,320]{1,0:T(8,128)(2,1)S(1)}, u32[]{:S(2)}) copy-start(bf16[512,320]{1,0:T(8,128)(2,1)S(1)} %collective-permute-done.10.d2) | copy-start | bytes 983044
  211.4 0.7 copy-start.12
  263.0 3.1 copy-start.6
  264.9 9.8 %collective-permute-start.13 = (bf16[512,1280]{1,0:T(8,128)(2,1)S(1)}, bf16[512,1280]{1,0:T(8,128)(2,1)}, u32[]{:S(2)}, u32[]{:S(2)}) collective-permute-start(bf16[512,1280]{1,0:T(8,128)(2,1)S(1)} %get-tuple-element.100), channel_id=1, source_target_pairs={{0,1},{1,0},{2,3},{3,2},{4,5},{5,4},{6,7},{7,6},{8,9},{9,8},{10,11... | collective-permute-start | bytes 3932168 | tf_op jit(solution)/shard_map/ppermute | solution.py:51
  266.1 6.1 %collective-permute-start.19 = (bf16[48,1280]{1,0:T(8,128)(2,1)S(1)}, bf16[48,1280]{1,0:T(8,128)(2,1)S(1)}, u32[]{:S(2)}, u32[]{:S(2)}) collective-permute-start(bf16[48,1280]{1,0:T(8,128)(2,1)S(1)} %slice.18), channel_id=1, source_target_pairs={{0,2},{1,3},{2,0},{3,1},{4,6},{5,7},{6,4},{7,5},{8,10},{9,11},{10,... | collective-permute-start | bytes 368648 | tf_op jit(solution)/shard_map/ppermute | solution.py:51
  267.6 4.6 %collective-permute-start.18 = (bf16[48,1280]{1,0:T(8,128)(2,1)S(1)}, bf16[48,1280]{1,0:T(8,128)(2,1)S(1)}, u32[]{:S(2)}, u32[]{:S(2)}) collective-permute-start(bf16[48,1280]{1,0:T(8,128)(2,1)S(1)} %slice.18), channel_id=1, source_target_pairs={{0,1},{1,0},{2,3},{3,2},{4,5},{5,4},{6,7},{7,6},{8,9},{9,8},{10,11... | collective-permute-start | bytes 368648 | tf_op jit(solution)/shard_map/ppermute | solution.py:51
  267.6 5.6 %collective-permute-start.20 = (bf16[48,1280]{1,0:T(8,128)(2,1)S(1)}, bf16[48,1280]{1,0:T(8,128)(2,1)S(1)}, u32[]{:S(2)}, u32[]{:S(2)}) collective-permute-start(bf16[48,1280]{1,0:T(8,128)(2,1)S(1)} %slice.18), channel_id=1, source_target_pairs={{0,3},{1,2},{2,1},{3,0},{4,7},{5,6},{6,5},{7,4},{8,11},{9,10},{10,... | collective-permute-start | bytes 368648 | tf_op jit(solution)/shard_map/ppermute | solution.py:51
  274.0 50.8 %collective-permute-start.12 = (bf16[512,1280]{1,0:T(8,128)(2,1)S(1)}, bf16[512,1280]{1,0:T(8,128)(2,1)}, u32[]{:S(2)}, u32[]{:S(2)}) collective-permute-start(bf16[512,1280]{1,0:T(8,128)(2,1)S(1)} %get-tuple-element.101), channel_id=1, source_target_pairs={{0,1},{1,0},{2,3},{3,2},{4,5},{5,4},{6,7},{7,6},{8,9},{9,8},{10,11... | collective-permute-start | bytes 3932168 | tf_op jit(solution)/shard_map/ppermute | solution.py:51
  277.8 47.0 %collective-permute-start.14 = (bf16[512,1280]{1,0:T(8,128)(2,1)}, bf16[512,1280]{1,0:T(8,128)(2,1)S(1)}, u32[]{:S(2)}, u32[]{:S(2)}) collective-permute-start(bf16[512,1280]{1,0:T(8,128)(2,1)} %fusion), channel_id=1, source_target_pairs={{0,2},{1,3},{2,0},{3,1},{4,6},{5,7},{6,4},{7,5},{8,10},{9,11},{10,... | collective-permute-start | bytes 3932168 | tf_op jit(solution)/shard_map/ppermute | solution.py:51
  324.8 1.1 copy-start
Sparse Core Ops, SparseCore 0:
  36.2 54.5 all-gather.5
  197.2 40.9 all-gather.7
  274.1 40.8 all-gather.9

commit v2 on v1

v2 whole, which is shorter than its diff:
```python
import functools
import math

import jax
import jax.numpy as jnp
from jax import lax
from jax.experimental import pallas as pl
from jax.experimental.pallas import tpu as pltpu
from jax.sharding import PartitionSpec as P

HD = 80
LANES = 128
EPS = 1e-06
NEG = -1e30
F32 = jnp.float32
BF16 = jnp.bfloat16
VMEM_BYTES = 60 * 2**20
SCORE_SCALE = HD ** (-0.5)
LOG2E = math.log2(math.e)
SLOT = 384

NT = (((1,), (1,)), ((), ()))
TN = (((0,), (0,)), ((), ()))


def nn(left, right):
    return jnp.dot(left, right, preferred_element_type=F32)


def nt(left, right):
    return lax.dot_general(left, right, NT, preferred_element_type=F32)


def tn(left, right):
    return lax.dot_general(left, right, TN, preferred_element_type=F32)


def params(**more):
    return pltpu.CompilerParams(vmem_limit_bytes=VMEM_BYTES, **more)


def cost(flops, nbytes):
    return pl.CostEstimate(flops=int(flops), bytes_accessed=int(nbytes), transcendentals=0)


def whole(shape):
    return pl.BlockSpec(shape, lambda *_: (0,) * len(shape))


def swap(array, axis_name, count, bit):
    return lax.ppermute(array, axis_name, [(i, i ^ bit) for i in range(count)])


def norm_kernel(choice, x_ref, ol_ref, ur_ref, dl_ref, out_ref):
    rows = x_ref.shape[0]
    x = x_ref[...].astype(F32)
    factor = lax.rsqrt(jnp.mean(x * x, axis=-1, keepdims=True) + EPS)
    out_ref[:rows] = (x * factor).astype(BF16)
    out_ref[rows:] = jnp.zeros_like(out_ref[rows:])
    width = ol_ref.shape[2]
    for slot, ref in enumerate((ol_ref, ur_ref, dl_ref)):
        out_ref[rows:, slot * SLOT : slot * SLOT + width] = ref[0]


def norm_call(x, choice, ol, ur, dl):
    rows, width = x.shape
    rank, local = ol.shape[1:]
    pick = pl.BlockSpec((1, rank, local), lambda g, c: (c[0], 0, 0))
    return pl.pallas_call(
        norm_kernel,
        grid_spec=pltpu.PrefetchScalarGridSpec(
            num_scalar_prefetch=1,
            grid=(1,),
            in_specs=[whole((rows, width)), pick, pick, pick],
            out_specs=whole((rows + rank, width)),
        ),
        out_shape=jax.ShapeDtypeStruct((rows + rank, width), BF16),
        compiler_params=params(),
        name="norm_in",
    )(choice, x, ol, ur, dl)


def copies_of(pieces, buf, sems):
    rows = buf.shape[1]
    return [
        pltpu.make_async_copy(piece.at[pl.ds(0, rows)], buf.at[n], sems.at[n])
        for n, piece in enumerate(pieces)
    ]


def bring(copies):
    step = pl.program_id(0)

    @pl.when(step == 0)
    def _():
        for c in copies:
            c.start()

    for n, c in enumerate(copies):

        @pl.when(step == n)
        def _(c=c):
            c.wait()


def project_step(heads, block, stack, raises, qt_ref, kt_ref, vt_ref, k_ref, v_ref, low_ref):
    width = heads * HD
    rank = raises[0].shape[1]
    out = nt(stack[...], block)
    low = out[3 * width :].astype(BF16)
    low_ref[...] = low
    for n, (r, col_ref, row_ref) in enumerate(
        zip(raises, (qt_ref, kt_ref, vt_ref), (None, k_ref, v_ref))
    ):
        part = out[n * width : (n + 1) * width] + tn(r[0], low[n * rank : (n + 1) * rank])
        if n == 0:
            part = part * (SCORE_SCALE * LOG2E)
        part = part.astype(BF16)
        col_ref[...] = part
        if row_ref is not None:
            for h in range(heads):
                at = h * LANES
                row_ref[:, at : at + HD] = part[h * HD : (h + 1) * HD].T


def project_near_kernel(
    heads, scal, p0, p1, wq, wk, wv, lq, lk, lv, rq, rk, rv,
    qt_ref, kt_ref, vt_ref, k_ref, v_ref, low_ref, stack, buf, sems,
):
    bring(copies_of((p0, p1), buf, sems))

    @pl.when(pl.program_id(0) == 0)
    def _():
        at = 0
        for part in (wq[...], wk[...], wv[...], lq[0], lk[0], lv[0]):
            stack[at : at + part.shape[0]] = part
            at += part.shape[0]

    project_step(
        heads, buf[pl.program_id(0)], stack, (rq, rk, rv),
        qt_ref, kt_ref, vt_ref, k_ref, v_ref, low_ref,
    )


def project_far_kernel(
    heads, scal, p0, p1, stack, rq, rk, rv, i0, i1, i2, i3, i4, i5,
    qt_ref, kt_ref, vt_ref, k_ref, v_ref, low_ref, buf, sems,
):
    bring(copies_of((p0, p1), buf, sems))
    project_step(
        heads, buf[pl.program_id(0)], stack, (rq, rk, rv),
        qt_ref, kt_ref, vt_ref, k_ref, v_ref, low_ref,
    )


def project_call(scal, first, pieces, weights, lowers, stack, raises, so_far, rows, length):
    depth = pieces[0].shape[1]
    rank, width = raises[0].shape[1:]
    heads = width // HD
    total = 3 * (width + rank)
    any_spec = pl.BlockSpec(memory_space=pl.ANY)
    lower = pl.BlockSpec((1, rank, depth), lambda g, s: (s[0], 0, 0))
    raise_ = pl.BlockSpec((1, rank, width), lambda g, s: (s[0], 0, 0))
    row = pl.BlockSpec((rows, heads * LANES), lambda g, s: (s[1] ^ (g + first), 0))
    col = pl.BlockSpec((width, rows), lambda g, s: (0, s[1] ^ (g + first)))
    low = pl.BlockSpec((3 * rank, rows), lambda g, s: (0, s[1] ^ (g + first)))
    col_t = jax.ShapeDtypeStruct((width, length), BF16)
    row_t = jax.ShapeDtypeStruct((length, heads * LANES), BF16)
    out_specs = [col, col, col, row, row, low]
    out_shape = [col_t, col_t, col_t, row_t, row_t, jax.ShapeDtypeStruct((3 * rank, length), BF16)]
    if so_far is None:
        body = project_near_kernel
        in_specs = [any_spec] * 2 + [whole((width, depth))] * 3 + [lower] * 3 + [raise_] * 3
        args = (*pieces, *weights, *lowers, *raises)
        out_specs = out_specs + [whole((total, depth))]
        out_shape = out_shape + [jax.ShapeDtypeStruct((total, depth), BF16)]
        alias = {}
    else:
        body = project_far_kernel
        in_specs = [any_spec] * 2 + [whole((total, depth))] + [raise_] * 3 + [any_spec] * 6
        args = (*pieces, stack, *raises, *so_far)
        alias = {7 + n: n for n in range(6)}
    return pl.pallas_call(
        functools.partial(body, heads),
        grid_spec=pltpu.PrefetchScalarGridSpec(
            num_scalar_prefetch=1,
            grid=(2,),
            in_specs=in_specs,
            out_specs=out_specs,
            scratch_shapes=[pltpu.VMEM((2, rows, depth), BF16), pltpu.SemaphoreType.DMA((2,))],
        ),
        out_shape=out_shape,
        input_output_aliases=alias,
        compiler_params=params(),
        cost_estimate=cost(2 * 2 * rows * depth * total, 16 * rows * depth),
        name="project",
    )(scal, *args)


def allowed_mask(seg_row, seg_col, last, start, size):
    key = lax.broadcasted_iota(jnp.int32, (last, size), 0)
    query = lax.broadcasted_iota(jnp.int32, (last, size), 1) + start
    return (seg_col[:last, :] == seg_row[:, start : start + size]) & (key <= query)


def attend_kernel(step, scal, seg_row, seg_col, qt_ref, k_ref, vt_ref, *rest):
    ot_ref, lse_ref, o0, o1, o2, o3, wide = rest[-7:]
    h = pl.program_id(0)
    length = qt_ref.shape[1]
    for i in range(length // step):
        start, last = i * step, (i + 1) * step
        s = nn(k_ref[:last, :HD], qt_ref[:, start:last])
        s = jnp.where(allowed_mask(seg_row, seg_col, last, start, step), s, NEG)
        top = jnp.max(s, axis=0, keepdims=True)
        p = jnp.exp2(s - top)
        total = jnp.sum(p, axis=0, keepdims=True)
        out = nn(vt_ref[:, :last], p.astype(BF16)) / total
        ot_ref[:, start:last] = out.astype(BF16)
        wide[pl.ds(pl.multiple_of(h * HD, 16), HD), start:last] = out
        lse_ref[0, :, start:last] = top + jnp.log2(total)

    @pl.when(h == pl.num_programs(0) - 1)
    def _():
        rows = o0.shape[0]
        for x, ref in enumerate((o0, o1, o2, o3)):
            at = pl.multiple_of((scal[1] ^ x) * rows, rows)
            ref[...] = wide[:, pl.ds(at, rows)].T.astype(BF16)


def attend_call(scal, seg_row, seg_col, qt, k, vt, first, count, so_far, rows):
    width, length = qt.shape
    heads = width // HD
    col = pl.BlockSpec((HD, length), lambda h, s: (h + first, 0))
    out = whole((rows, count * HD))
    out_t = jax.ShapeDtypeStruct((rows, count * HD), BF16)
    kept = [] if so_far is None else list(so_far)
    return pl.pallas_call(
        functools.partial(attend_kernel, 512),
        grid_spec=pltpu.PrefetchScalarGridSpec(
            num_scalar_prefetch=1,
            grid=(count,),
            in_specs=[
                whole((1, length)), whole((length, 1)), col,
                pl.BlockSpec((length, LANES), lambda h, s: (0, h + first)), col,
            ]
            + [pl.BlockSpec(memory_space=pl.ANY)] * len(kept),
            out_specs=[
                col,
                pl.BlockSpec((1, 1, length), lambda h, s: (h + first, 0, 0)),
                out, out, out, out,
            ],
            scratch_shapes=[pltpu.VMEM((count * HD, length), F32)],
        ),
        out_shape=[
            jax.ShapeDtypeStruct((width, length), BF16),
            jax.ShapeDtypeStruct((heads, 1, length), F32),
            out_t, out_t, out_t, out_t,
        ],
        input_output_aliases={6 + n: n for n in range(len(kept))},
        compiler_params=params(),
        cost_estimate=cost(count * 4 * length * length * LANES, 8 * length * count * LANES),
        name="attend",
    )(scal, seg_row, seg_col, qt, k, vt, *kept)


def attend_back_kernel(
    step, scal, seg_row, seg_col, qt_ref, kt_ref, k_ref, v_ref, ot_ref, lse_ref,
    d0, d1, d2, d3, dq_ref, dk_ref, dv_ref, grad_t, dk_sum, dv_sum,
):
    h = pl.program_id(0)
    length = qt_ref.shape[1]

    @pl.when(h == 0)
    def _():
        rows = d0.shape[0]
        for x, ref in enumerate((d0, d1, d2, d3)):
            at = pl.multiple_of((scal[1] ^ x) * rows, rows)
            grad_t[:, pl.ds(at, rows)] = ref[...].astype(F32).T.astype(BF16)

    mine = grad_t[pl.ds(pl.multiple_of(h * HD, 16), HD), :]
    row_dot = jnp.sum(mine.astype(F32) * ot_ref[...].astype(F32), axis=0, keepdims=True)
    for i in range(length // step):
        start, last = i * step, (i + 1) * step
        grad, query = mine[:, start:last], qt_ref[:, start:last]
        s = nn(k_ref[:last, :HD], query)
        dp = nn(v_ref[:last, :HD], grad)
        s = jnp.where(allowed_mask(seg_row, seg_col, last, start, step), s, NEG)
        p = jnp.exp2(s - lse_ref[0, :, start:last])
        ds = (p * (dp - row_dot[:, start:last])).astype(BF16)
        dv = nt(grad, p.astype(BF16))
        dk = nt(query, ds)
        dq = nn(kt_ref[:, :last], ds)
        if start:
            dv_sum[:, :start] += dv[:, :start]
            dk_sum[:, :start] += dk[:, :start]
        dv_sum[:, start:last] = dv[:, start:]
        dk_sum[:, start:last] = dk[:, start:]
        dq_ref[:, start:last] = (dq * SCORE_SCALE).astype(BF16)
    dk_ref[...] = (dk_sum[...] * (1.0 / LOG2E)).astype(BF16)
    dv_ref[...] = dv_sum[...].astype(BF16)


def attend_back_call(scal, seg_row, seg_col, qt, kt, k, v, ot, lse, grads):
    width, length = qt.shape
    heads = width // HD
    rows = grads[0].shape[0]
    row = pl.BlockSpec((length, LANES), lambda h, s: (0, h))
    col = pl.BlockSpec((HD, length), lambda h, s: (h, 0))
    col_t = jax.ShapeDtypeStruct((width, length), BF16)
    return pl.pallas_call(
        functools.partial(attend_back_kernel, 256),
        grid_spec=pltpu.PrefetchScalarGridSpec(
            num_scalar_prefetch=1,
            grid=(heads,),
            in_specs=[
                whole((1, length)), whole((length, 1)), col, col, row, row, col,
                pl.BlockSpec((1, 1, length), lambda h, s: (h, 0, 0)),
            ]
            + [whole((rows, width))] * 4,
            out_specs=[col, col, col],
            scratch_shapes=[
                pltpu.VMEM((width, length), BF16),
                pltpu.VMEM((HD, length), F32),
                pltpu.VMEM((HD, length), F32),
            ],
        ),
        out_shape=[col_t, col_t, col_t],
        compiler_params=params(),
        cost_estimate=cost(heads * 8 * length * length * LANES, 16 * length * width),
        name="attend_back",
    )(scal, seg_row, seg_col, qt, kt, k, v, ot, lse, *grads)


def middle_kernel(
    scal, x_ref, g_ref, a0, a1, a2, a3, b0, b1, b2, b3, s0, s1, s2, s3, w0, w1, w2, w3,
    orr, ulr, drr,
    act_ref, gm_ref, o0, o1, o2, o3, e0, e1, e2, e3,
    wo, wu, wd, ol, ur, dl, sems,
):
    width = o0.shape[1]
    rank = orr.shape[1]
    copies = []
    for n, dst in enumerate((wo, wu, wd)):
        for x, src in enumerate((w0, w1, w2, w3)):
            copies.append(
                pltpu.make_async_copy(
                    src.at[pl.ds(n * width, width)],
                    dst.at[pl.ds(x * width, width)],
                    sems.at[n * 4 + x],
                )
            )
    for copy in copies:
        copy.start()

    def arrived(n):
        for copy in copies[4 * n : 4 * n + 4]:
            copy.wait()

    for x, src in enumerate((s0, s1, s2, s3)):
        for slot, dst in enumerate((ol, ur, dl)):
            dst[:, x * width : (x + 1) * width] = src[:, slot * SLOT : slot * SLOT + width].astype(F32)
    out_lower, up_raise, down_lower = (r[...].astype(BF16) for r in (ol, ur, dl))
    out_raise, up_lower, down_raise = orr[0], ulr[0], drr[0]
    grad = g_ref[...]
    parts = [r[...].astype(F32) for r in (a0, b0, a1, b1, a2, b2, a3, b3)]
    att = jnp.concatenate(parts, axis=1).astype(BF16)
    low_out = nt(att, out_lower).astype(BF16)
    grad_low_down = nt(grad, down_raise).astype(BF16)
    arrived(0)
    middle = x_ref[...].astype(F32) + (nn(att, wo[...]) + nn(low_out, out_raise))
    factor = lax.rsqrt(jnp.mean(middle * middle, axis=-1, keepdims=True) + EPS)
    unit = middle * factor
    normed = unit.astype(BF16)
    low_up = nt(normed, up_lower).astype(BF16)
    arrived(1)
    preact = nt(normed, wu[...]) + nn(low_up, up_raise)
    sigma = 1.0 / (1.0 + jnp.exp(-preact))
    active = (preact * sigma).astype(BF16)
    arrived(2)
    low_down = nt(active, down_lower).astype(BF16)
    grad_act = nt(grad, wd[...]) + nn(grad_low_down, down_lower)
    grad_pre = (grad_act * (sigma * (1.0 + preact * (1.0 - sigma)))).astype(BF16)
    grad_low_up = nt(grad_pre, up_raise).astype(BF16)
    grad_mid = nn(grad_pre, wu[...]) + nn(grad_low_up, up_lower)
    act_ref[...] = (middle + (nn(active, wd[...]) + nn(low_down, down_raise))).astype(BF16)
    dot = jnp.mean(grad_mid * unit, axis=-1, keepdims=True)
    grad_middle = grad.astype(F32) + factor * (grad_mid - unit * dot)
    gm_ref[...] = grad_middle
    grad_attn = grad_middle.astype(BF16)
    grad_low_out = nt(grad_attn, out_raise).astype(BF16)
    grad_att = nt(grad_attn, wo[...]) + nn(grad_low_out, out_lower)
    for x, ref in enumerate((o0, o1, o2, o3)):
        ref[...] = grad_att[:, x * width : (x + 1) * width].astype(BF16)

    packs = (e0, e1, e2, e3)
    for n, (low, value) in enumerate(
        ((low_out, grad_attn), (grad_low_up, normed), (low_down, grad))
    ):
        part = tn(low, value).astype(BF16)
        for ref in packs:
            ref[n * rank : (n + 1) * rank] = part
    for x, ref in enumerate(packs):
        mark = jnp.full((rank, ref.shape[1]), scal[0], jnp.int32).astype(F32)
        ref[3 * rank :] = (jnp.zeros_like(mark) if x else mark).astype(BF16)
    for slot, (low, value) in enumerate(
        ((grad_low_out, att), (low_up, grad_pre), (grad_low_down, active))
    ):
        part = tn(low, value)
        for x, ref in enumerate(packs):
            piece = part[:, x * width : (x + 1) * width].astype(BF16)
            ref[3 * rank :, slot * SLOT : slot * SLOT + width] = piece


def middle_call(scal, x, g, att, pieces, weights, out_raise, up_lower, down_raise):
    rows, depth = x.shape
    width = 2 * att[0].shape[1]
    rank = out_raise.shape[1]
    wide = whole((rows, depth))
    part = whole((rows, width))
    small = pl.BlockSpec((rank, depth), lambda c, s: (rows // rank, 0))
    pick = pl.BlockSpec((1, rank, depth), lambda c, s: (s[0], 0, 0))
    any_spec = pl.BlockSpec(memory_space=pl.ANY)
    part_t = jax.ShapeDtypeStruct((rows, width), BF16)
    pack_t = jax.ShapeDtypeStruct((4 * rank, depth), BF16)
    square = pltpu.VMEM((4 * width, depth), BF16)
    thin = pltpu.VMEM((rank, depth), F32)
    return pl.pallas_call(
        middle_kernel,
        grid_spec=pltpu.PrefetchScalarGridSpec(
            num_scalar_prefetch=1,
            grid=(1,),
            in_specs=[wide, wide] + [whole((rows, width // 2))] * 8 + [small] * 4
            + [any_spec] * 4 + [pick] * 3,
            out_specs=[wide, wide] + [part] * 4 + [whole((4 * rank, depth))] * 4,
            scratch_shapes=[
                square, square, square, thin, thin, thin,
                pltpu.SemaphoreType.DMA((12,)),
            ],
        ),
        out_shape=[
            jax.ShapeDtypeStruct((rows, depth), BF16),
            jax.ShapeDtypeStruct((rows, depth), F32),
        ]
        + [part_t] * 4
        + [pack_t] * 4,
        compiler_params=params(),
        cost_estimate=cost(12 * rows * depth * depth, 6 * depth * depth + 12 * rows * depth),
        name="feed_forward",
    )(scal, x, g, *att, *pieces, *weights, out_raise, up_lower, down_raise)


def adapter_kernel(
    scal, dq, dk, dv, low, p0, p1, p2, p3, rq, rk, rv,
    back_ref, pack_ref, buf, sems, lower_sum, raise_sum,
):
    step = pl.program_id(0)
    bring(copies_of((p0, p1, p2, p3), buf, sems))

    @pl.when(step == 0)
    def _():
        lower_sum[...] = jnp.zeros_like(lower_sum)
        raise_sum[...] = jnp.zeros_like(raise_sum)

    rank, width = rq.shape[1:]
    parts = []
    for n, (d, r) in enumerate(((dq, rq), (dk, rk), (dv, rv))):
        value = d[...]
        parts.append(nn(r[0], value))
        raise_sum[:, n * SLOT : n * SLOT + width] += nt(low[n * rank : (n + 1) * rank], value)
    back = jnp.concatenate(parts, axis=0).astype(BF16)
    back_ref[...] = back
    lower_sum[...] += nn(back, buf[step])

    @pl.when(step == pl.num_programs(0) - 1)
    def _():
        pack_ref[: 3 * rank] = lower_sum[...].astype(BF16)
        pack_ref[3 * rank :] = raise_sum[...].astype(BF16)


def adapter_call(scal, grads, low, pieces, raises, rows):
    depth = pieces[0].shape[1]
    width, length = grads[0].shape
    rank = raises[0].shape[1]
    any_spec = pl.BlockSpec(memory_space=pl.ANY)
    raise_ = pl.BlockSpec((1, rank, width), lambda g, s: (s[0], 0, 0))
    col = pl.BlockSpec((width, rows), lambda g, s: (0, s[1] ^ g))
    thin = pl.BlockSpec((3 * rank, rows), lambda g, s: (0, s[1] ^ g))
    return pl.pallas_call(
        adapter_kernel,
        grid_spec=pltpu.PrefetchScalarGridSpec(
            num_scalar_prefetch=1,
            grid=(4,),
            in_specs=[col] * 3 + [thin] + [any_spec] * 4 + [raise_] * 3,
            out_specs=[thin, whole((4 * rank, depth))],
            scratch_shapes=[
                pltpu.VMEM((4, rows, depth), BF16),
                pltpu.SemaphoreType.DMA((4,)),
                pltpu.VMEM((3 * rank, depth), F32),
                pltpu.VMEM((rank, depth), F32),
            ],
        ),
        out_shape=[
            jax.ShapeDtypeStruct((3 * rank, length), BF16),
            jax.ShapeDtypeStruct((4 * rank, depth), BF16),
        ],
        compiler_params=params(),
        cost_estimate=cost(8 * length * depth * 3 * rank, 4 * length * depth),
        name="adapter_gradients",
    )(scal, *grads, low, *pieces, *raises)


def grad_in_kernel(scal, dq, dk, dv, back, stack, out_ref):
    value = jnp.concatenate([dq[...], dk[...], dv[...], back[...]], axis=0)
    out_ref[0] = tn(value, stack[...]).astype(BF16)


def grad_in_call(scal, grads, back, stack, first, rows):
    width = grads[0].shape[0]
    total, depth = stack.shape
    col = pl.BlockSpec((width, rows), lambda g, s: (0, s[1] ^ (g + first)))
    thin = pl.BlockSpec((back.shape[0], rows), lambda g, s: (0, s[1] ^ (g + first)))
    return pl.pallas_call(
        grad_in_kernel,
        grid_spec=pltpu.PrefetchScalarGridSpec(
            num_scalar_prefetch=1,
            grid=(2,),
            in_specs=[col] * 3 + [thin, whole((total, depth))],
            out_specs=pl.BlockSpec((1, rows, depth), lambda g, s: (g, 0, 0)),
        ),
        out_shape=jax.ShapeDtypeStruct((2, rows, depth), BF16),
        compiler_params=params(),
        cost_estimate=cost(4 * rows * depth * total, 12 * rows * depth),
        name="grad_input",
    )(scal, *grads, back, stack)


def last_kernel(x_ref, gm_ref, a_ref, b_ref, c_ref, out_ref):
    x = x_ref[...].astype(F32)
    factor = lax.rsqrt(jnp.mean(x * x, axis=-1, keepdims=True) + EPS)
    unit = x * factor
    grad = a_ref[0].astype(F32) + b_ref[...].astype(F32) + c_ref[...].astype(F32)
    dot = jnp.mean(grad * unit, axis=-1, keepdims=True)
    out_ref[...] = (gm_ref[...] + factor * (grad - unit * dot)).astype(BF16)


def last_call(x, gm, a, b, c):
    rows, depth = x.shape
    step = 128
    wide = pl.BlockSpec((step, depth), lambda g: (g, 0))
    return pl.pallas_call(
        last_kernel,
        grid=(rows // step,),
        in_specs=[wide, wide, pl.BlockSpec((1, step, depth), lambda g: (0, g, 0)), wide, wide],
        out_specs=wide,
        out_shape=jax.ShapeDtypeStruct((rows, depth), BF16),
        compiler_params=params(),
        name="input_gradient",
    )(x, gm, a, b, c)


def sets_kernel(mark_ref, pack_ref, *outs):
    j = pl.program_id(0)
    rank = outs[0].shape[1]
    depth = mark_ref.shape[2]
    total = jnp.zeros(pack_ref.shape[1:], F32)
    for n in range(pack_ref.shape[0]):
        chosen = mark_ref[n, 3 * rank : 3 * rank + 1, depth - 1 : depth].astype(F32)
        pick = (chosen == j.astype(F32)).astype(F32)
        total = total + pack_ref[n].astype(F32) * pick
    for k in range(3):
        outs[k][0] = total[k * rank : (k + 1) * rank]
        width = outs[3 + k].shape[2]
        outs[3 + k][0] = total[3 * rank :, k * SLOT : k * SLOT + width]


def sets_call(marks, packs, sets, width):
    parts, four, depth = packs.shape
    rank = four // 4
    full = pl.BlockSpec((1, rank, depth), lambda j: (j, 0, 0))
    thin = pl.BlockSpec((1, rank, width), lambda j: (j, 0, 0))
    full_t = jax.ShapeDtypeStruct((sets, rank, depth), F32)
    thin_t = jax.ShapeDtypeStruct((sets, rank, width), F32)
    return pl.pallas_call(
        sets_kernel,
        grid=(sets,),
        in_specs=[whole(marks.shape), whole(packs.shape)],
        out_specs=[full, full, full, thin, thin, thin],
        out_shape=[full_t, full_t, full_t, thin_t, thin_t, thin_t],
        compiler_params=params(),
        name="set_sums",
    )(marks, packs)


def on_device(
    dp_count,
    tensor_count,
    tokens,
    segment_ids,
    adapter_choice,
    cotangent,
    weight_query,
    weight_key,
    weight_value,
    weight_output,
    weight_upward,
    weight_downward,
    query_lower,
    query_raise,
    key_lower,
    key_raise,
    value_lower,
    value_raise,
    output_lower,
    output_raise,
    upward_lower,
    upward_raise,
    downward_lower,
    downward_raise,
):
    across = functools.partial(swap, axis_name="tensor", count=tensor_count)
    x, g = tokens[0], cotangent[0]
    rows = x.shape[0]
    length = segment_ids.shape[1]
    sets, rank = query_lower.shape[:2]
    me = lax.axis_index("tensor").astype(jnp.int32)
    scal = jnp.stack([adapter_choice[0], me])
    seg_row = segment_ids
    seg_col = segment_ids.reshape(length, 1)

    own = norm_call(x, adapter_choice, output_lower, upward_raise, downward_lower)
    far = across(own, bit=2)
    near = across(own, bit=1)
    out_t, up_t, down_t, own = lax.optimization_barrier(
        (weight_output.T, weight_upward.T, weight_downward.T, own)
    )
    wt = jnp.concatenate([out_t, up_t, down_t], axis=0)
    share = wt.shape[0] // dp_count
    mine = lax.dynamic_slice_in_dim(wt, lax.axis_index("dp") * share, share, 0)
    fetched = across(mine, bit=2)
    wt_far = lax.all_gather(fetched, "dp", axis=0, tiled=True)
    wt_near = across(wt, bit=1)

    lowers = (query_lower, key_lower, value_lower)
    raises = (query_raise, key_raise, value_raise)
    weights = (weight_query.T, weight_key.T, weight_value.T)
    *so_far, stack = project_call(
        scal, 0, (own, near), weights, lowers, None, raises, None, rows, length
    )
    cross = across(far, bit=1)
    pieces = (own, near, far, cross)
    qt, kt, vt, k, v, low = project_call(
        scal, 2, (far, cross), None, None, stack, raises, so_far, rows, length
    )
    heads = qt.shape[0] // HD
    half = heads // 2
    ot, lse, *att = attend_call(scal, seg_row, seg_col, qt, k, vt, 0, half, None, rows)
    left = [att[0]] + [across(att[n], bit=n) for n in (1, 2, 3)]
    ot, lse, *att = attend_call(scal, seg_row, seg_col, qt, k, vt, half, half, (ot, lse), rows)
    wt_far, att[0] = lax.optimization_barrier((wt_far, att[0]))
    wt_cross = across(wt_far, bit=1)
    right = [att[0]] + [across(att[n], bit=n) for n in (1, 2, 3)]
    act, grad_middle, *more = middle_call(
        scal, x, g, (*left, *right), pieces, (wt, wt_near, wt_far, wt_cross),
        output_raise, upward_lower, downward_raise,
    )
    grads, packs = more[:4], more[4:]
    grads = [grads[0]] + [across(grads[n], bit=n) for n in (1, 2, 3)]
    back = attend_back_call(scal, seg_row, seg_col, qt, kt, k, v, ot, lse, grads)

    packs = [packs[0]] + [across(packs[n], bit=n) for n in (1, 2, 3)]
    packs = [p.astype(F32) for p in packs]
    first = ((packs[0] + packs[1]) + (packs[2] + packs[3])).astype(BF16)
    first_all = lax.all_gather(first, "dp", axis=0)

    low_back, pack = adapter_call(scal, back, low, pieces, raises, rows)
    lower_part = pack[: 3 * rank]
    others = [across(lower_part, bit=n).astype(F32) for n in (1, 2, 3)]
    lower_sum = (lower_part.astype(F32) + others[0]) + (others[1] + others[2])
    second = jnp.concatenate([lower_sum.astype(BF16), pack[3 * rank :]], axis=0)
    second_all = lax.all_gather(second, "dp", axis=0)

    partial_far = grad_in_call(scal, back, low_back, stack, 2, rows)
    near_far = across(partial_far[1], bit=1)
    to_far = (partial_far[0].astype(F32) + near_far.astype(F32)).astype(BF16)
    from_far = across(to_far, bit=2)
    partial = grad_in_call(scal, back, low_back, stack, 0, rows)
    near_mine = across(partial[1], bit=1)
    input_grad = last_call(x, grad_middle, partial, near_mine, from_far)

    out = list(sets_call(first_all, first_all, sets, query_raise.shape[2]))
    out += sets_call(first_all, second_all, sets, query_raise.shape[2])
    (out_raise_g, up_lower_g, down_raise_g, out_lower_g, up_raise_g, down_lower_g) = out[:6]
    (q_lower_g, k_lower_g, v_lower_g, q_raise_g, k_raise_g, v_raise_g) = out[6:]
    return (
        act[None],
        input_grad[None],
        q_lower_g,
        q_raise_g,
        k_lower_g,
        k_raise_g,
        v_lower_g,
        v_raise_g,
        out_lower_g,
        out_raise_g,
        up_lower_g,
        up_raise_g,
        down_lower_g,
        down_raise_g,
    )


def solution(mesh):
    split = P(None, None, "tensor")
    return jax.shard_map(
        functools.partial(on_device, mesh.shape["dp"], mesh.shape["tensor"]),
        mesh=mesh,
        in_specs=(
            P("dp", "tensor", None),
            P("dp", None),
            P("dp"),
            P("dp", "tensor", None),
            P(None, "tensor"),
            P(None, "tensor"),
            P(None, "tensor"),
            P(None, "tensor"),
            P(None, "tensor"),
            P(None, "tensor"),
            P(),
            split,
            P(),
            split,
            P(),
            split,
            split,
            P(),
            P(),
            split,
            split,
            P(),
        ),
        out_specs=(
            P("dp", "tensor", None),
            P("dp", "tensor", None),
            P(),
            split,
            P(),
            split,
            P(),
            split,
            split,
            P(),
            P(),
            split,
            split,
            P(),
        ),
        check_vma=False,
    )
```

time: 338 us -> 317 us (0.938); the launches traced: 338 us -> 313 us
  waiting for transfers between devices: 135 us -> 109 us
    all_gather x1, waiting for transfers between devices: 19.4 us -> 0.02 us  [on_device(): wt_far = lax.all_gather(fetched, 'dp', axis=0, tiled=True)]
    all_gather x1, waiting for transfers between devices: 35.8 us -> 30.5 us  [on_device(): second_all = lax.all_gather(second, 'dp', axis=0)]
    pallas_call x4 -> x7, Pallas kernels: 58.2 us -> 53.3 us  [the longest x2 19.5 us: project_call(): pl.pallas_call(functools.partial(body, heads), grid_spec=pltpu.PrefetchSc...]
    unnamed x38 -> x46, local copies, waits for them, and re-layouts: 12.1 us -> 8.41 us
    pallas_call x1 -> x2, Pallas kernels: 20.7 us -> 24.1 us  [attend_call(): pl.pallas_call(functools.partial(attend_kernel, 512), grid_spec=pltpu.Pre...]
    ppermute x21 -> x24, waiting for transfers between devices: 79.5 us -> 78 us  [swap(): return lax.ppermute(array, axis_name, [(i, i ^ bit) for i in range(count)])]
    ppermute x21 -> x24, starting transfers between devices: 17.2 us -> 18 us  [swap(): return lax.ppermute(array, axis_name, [(i, i ^ bit) for i in range(count)])]
  transfers between devices with their start and end apart: 24 -> 27, of which waited for: 13 -> 12; matrix products, arithmetic and copies ran while one was open for 3% -> 4% of each run, Pallas kernels for 31% -> 34%
where the time goes in v2:
time: 317 us; the launch traced here: 313 us
  Pallas kernels  148 us (47%)
  waiting for transfers between devices  109 us (34%)
  starting transfers between devices  18.1 us (6%)
  local copies, waits for them, and re-layouts  17.7 us (6%)
  between operations  14.8 us (5%)
  other arithmetic  5.69 us (2%)
    ppermute x24, waiting for transfers between devices, swap(): return lax.ppermute(array, axis_name, [(i, i ^ bit) for i in range(count)])  78 us
    pallas_call x1, Pallas kernels, middle_call(): pl.pallas_call(middle_kernel, grid_spec=pltpu.PrefetchScalarGridSpec(num_...  33 us
    all_gather x1, waiting for transfers between devices, on_device(): second_all = lax.all_gather(second, 'dp', axis=0)  30.5 us
    pallas_call x1, Pallas kernels, attend_back_call(): pl.pallas_call(functools.partial(attend_back_kernel, 256), grid_spec=pltp...  29 us
    pallas_call x2, Pallas kernels, attend_call(): pl.pallas_call(functools.partial(attend_kernel, 512), grid_spec=pltpu.Pre...  24.1 us
    pallas_call x2, Pallas kernels, project_call(): pl.pallas_call(functools.partial(body, heads), grid_spec=pltpu.PrefetchSc...  19.5 us
    ppermute x24, starting transfers between devices, swap(): return lax.ppermute(array, axis_name, [(i, i ^ bit) for i in range(count)])  18 us
    pallas_call x2, Pallas kernels, grad_in_call(): pl.pallas_call(grad_in_kernel, grid_spec=pltpu.PrefetchScalarGridSpec(num...  14.3 us
  transfers between devices with their start and end apart: 27, of which 12 were waited for; matrix products, arithmetic and copies ran while one was open for 4% of the time, Pallas kernels for 34%

profile of v2, /device:TPU:0, one launch (start us, length us, event | category | flops | bytes accessed | tf_op | source)
XLA Modules:
  0.0 312.6 jit_solution(12372386636243731005)
XLA Ops:
  7.9 2.9 norm_in.1.p0.s0
  10.8 1.0 constant_dynamic-update-slice_fusion.2
  11.8 0.5 copy-done.5
  12.3 1.0 constant_dynamic-update-slice_fusion.1
  13.2 1.0 constant_dynamic-update-slice_fusion.w0
  14.2 1.0 constant_dynamic-slice_fusion
  15.2 3.0 collective-permute-start.6
  18.2 7.3 %collective-permute-done.6 = bf16[120,1280]{1,0:T(8,128)(2,1)S(1)} collective-permute-done((bf16[120,1280]{1,0:T(8,128)(2,1)S(1)}, bf16[120,1280]{1,0:T(8,128)(2,1)S(1)}, u32[]{:S(2)}, u32[]{:S(2)}) %collective-permute-start.6) | collective-permute-done | bytes 307232 | tf_op jit(solution)/shard_map/ppermute | solution.py:51
  25.5 0.7 copy-done.8
  26.2 0.0 all-gather.8.cloned.1.call-start
  26.3 1.8 collective-permute-start
  28.1 29.3 %collective-permute-done.p0.s2.p2 = bf16[528,1280]{1,0:T(8,128)(2,1)S(1)} collective-permute-done((bf16[528,1280]{1,0:T(8,128)(2,1)}, bf16[528,1280]{1,0:T(8,128)(2,1)S(1)}, u32[]{:S(2)}, u32[]{:S(2)}) %collective-permute-start) | collective-permute-done | bytes 1351712 | tf_op jit(solution)/shard_map/ppermute | solution.py:51
  57.4 0.5 collective-permute-start.10
  57.9 1.4 copy.44.seg_col
  59.3 0.6 pad_add_fusion.scal
  59.8 10.3 %project.2 = (bf16[320,2048]{1,0:T(8,128)(2,1)}, bf16[320,2048]{1,0:T(8,128)(2,1)}, bf16[320,2048]{1,0:T(8,128)(2,1)}, bf16[2048,512]{1,0:T(8,128)(2,1)}, bf16[2...) custom-call(s32[2]{0:T(128)} %pad_add_fusion.scal, bf16[528,1280]{1,0:T(8,128)(2,1)} %norm_in.1.p0.s0, ...), custom_call_target="tpu_custom_call" | custom-call | flops 2642411520 | bytes 10485760 | tf_op jit(solution)/shard_map/project/pallas_call | solution.py:183
  70.1 1.2 copy-done.1
  71.3 9.2 %project.3 = (bf16[320,2048]{1,0:T(8,128)(2,1)}, bf16[320,2048]{1,0:T(8,128)(2,1)}, bf16[320,2048]{1,0:T(8,128)(2,1)}, bf16[2048,512]{1,0:T(8,128)(2,1)}, bf16[2...) custom-call(s32[2]{0:T(128)} %pad_add_fusion.scal, ...), custom_call_target="tpu_custom_call", output_to_operand_aliasing={{0}: (7, {}), {1}: (8, {}), {2}: (9, {}), {3}: (10, {}), {4... | custom-call | flops 2642411520 | bytes 10485760 | tf_op jit(solution)/shard_map/project/pallas_call | solution.py:183
  80.6 11.9 %attend.2 = (bf16[320,2048]{1,0:T(8,128)(2,1)}, f32[4,1,2048]{2,1,0:T(1,128)}, bf16[512,160]{1,0:T(8,128)(2,1)}, bf16[512,160]{1,0:T(8,128)(2,1)}, bf16[512,160]{1,0:T(8,128)(2,1)}, /*index=5*/bf16[512,160]{1,0:T(8,128)(2,1)}) custom-call(s32[2]{0:T(128)} %pad_add_fusion.scal, s32[1,2048]{1,0:T(1,128)} %seg_row.5, s32[2048,1]{1,0:T(8,128)} %copy.44.seg_col, ...), custom_call_target="tpu_custom_call" | custom-call | flops 4294967296 | bytes 4194304 | tf_op jit(solution)/shard_map/attend/pallas_call | solution.py:237
  92.5 12.2 %attend.3 = (bf16[320,2048]{1,0:T(8,128)(2,1)}, f32[4,1,2048]{2,1,0:T(1,128)}, bf16[512,160]{1,0:T(8,128)(2,1)}, bf16[512,160]{1,0:T(8,128)(2,1)}, bf16[512,160]{1,0:T(8,128)(2,1)}, /*index=5*/bf16[512,160]{1,0:T(8,128)(2,1)}) custom-call(s32[2]{0:T(128)} %pad_add_fusion.scal, s32[1,2048]{1,0:T(1,128)} %seg_row.5, ...), custom_call_target="tpu_custom_call", output_to_operand_aliasing={{0}: (6, {}), {1}: (7, {})} | custom-call | flops 4294967296 | bytes 4194304 | tf_op jit(solution)/shard_map/attend/pallas_call | solution.py:237
  104.7 0.1 collective-permute-start.11
  104.8 0.5 collective-permute-start.3
  105.3 1.4 collective-permute-start.4
  106.7 0.7 collective-permute-start.7
  107.4 2.4 collective-permute-done.3.a1
  109.8 1.4 collective-permute-start.8
  111.3 3.4 %collective-permute-done.4.a2 = bf16[512,160]{1,0:T(8,128)(2,1)S(1)} collective-permute-done((bf16[512,160]{1,0:T(8,128)(2,1)}, bf16[512,160]{1,0:T(8,128)(2,1)S(1)}, u32[]{:S(2)}, u32[]{:S(2)}) %collective-permute-start.4) | collective-permute-done | bytes 163872 | tf_op jit(solution)/shard_map/ppermute | solution.py:51
  114.7 4.5 %collective-permute-done.5.a3 = bf16[512,160]{1,0:T(8,128)(2,1)S(1)} collective-permute-done((bf16[512,160]{1,0:T(8,128)(2,1)S(1)}, bf16[512,160]{1,0:T(8,128)(2,1)S(1)}, u32[]{:S(2)}, u32[]{:S(2)}) %collective-permute-start.5) | collective-permute-done | bytes 163872 | tf_op jit(solution)/shard_map/ppermute | solution.py:51
  119.2 6.7 %collective-permute-done.8.b2 = bf16[512,160]{1,0:T(8,128)(2,1)S(1)} collective-permute-done((bf16[512,160]{1,0:T(8,128)(2,1)}, bf16[512,160]{1,0:T(8,128)(2,1)S(1)}, u32[]{:S(2)}, u32[]{:S(2)}) %collective-permute-start.8) | collective-permute-done | bytes 163872 | tf_op jit(solution)/shard_map/ppermute | solution.py:51
  125.9 3.9 %collective-permute-done.9.b3 = bf16[512,160]{1,0:T(8,128)(2,1)S(1)} collective-permute-done((bf16[512,160]{1,0:T(8,128)(2,1)}, bf16[512,160]{1,0:T(8,128)(2,1)S(1)}, u32[]{:S(2)}, u32[]{:S(2)}) %collective-permute-start.9) | collective-permute-done | bytes 163872 | tf_op jit(solution)/shard_map/ppermute | solution.py:51
  129.8 0.7 copy-done.20
  130.5 1.5 copy-done.10
  132.0 33.0 %feed_forward.1 = (bf16[512,1280]{1,0:T(8,128)(2,1)}, f32[512,1280]{1,0:T(8,128)}, bf16[512,320]{1,0:T(8,128)(2,1)}, bf16[512,320]{1,0:T(8,128)(2,1)}, bf16[512,...) custom-call(s32[2]{0:T(128)} %pad_add_fusion.scal, ...), custom_call_target="tpu_custom_call" | custom-call | flops 10066329600 | bytes 17694720 | tf_op jit(solution)/shard_map/feed_forward/pallas_call | solution.py:427
  165.0 0.8 collective-permute-start.18
  165.8 1.4 collective-permute-start.19
  167.2 0.7 collective-permute-start.12
  167.9 1.4 collective-permute-start.13
  169.3 3.7 %collective-permute-done.19 = bf16[64,1280]{1,0:T(8,128)(2,1)S(1)} collective-permute-done((bf16[64,1280]{1,0:T(8,128)(2,1)}, bf16[64,1280]{1,0:T(8,128)(2,1)S(1)}, u32[]{:S(2)}, u32[]{:S(2)}) %collective-permute-start.19) | collective-permute-done | bytes 163872 | tf_op jit(solution)/shard_map/ppermute | solution.py:51
  173.0 2.6 collective-permute-done.20
  175.6 1.7 add_convert_fusion
  177.4 7.6 %collective-permute-done.13.d2 = bf16[512,320]{1,0:T(8,128)(2,1)S(1)} collective-permute-done((bf16[512,320]{1,0:T(8,128)(2,1)}, bf16[512,320]{1,0:T(8,128)(2,1)S(1)}, u32[]{:S(2)}, u32[]{:S(2)}) %collective-permute-start.13) | collective-permute-done | bytes 327712 | tf_op jit(solution)/shard_map/ppermute | solution.py:51
  185.0 6.7 %collective-permute-done.14.d3 = bf16[512,320]{1,0:T(8,128)(2,1)S(1)} collective-permute-done((bf16[512,320]{1,0:T(8,128)(2,1)}, bf16[512,320]{1,0:T(8,128)(2,1)S(1)}, u32[]{:S(2)}, u32[]{:S(2)}) %collective-permute-start.14) | collective-permute-done | bytes 327712 | tf_op jit(solution)/shard_map/ppermute | solution.py:51
  191.7 0.7 copy-done.13
  192.4 29.0 %attend_back.1 = (bf16[320,2048]{1,0:T(8,128)(2,1)}, bf16[320,2048]{1,0:T(8,128)(2,1)}, bf16[320,2048]{1,0:T(8,128)(2,1)}) custom-call(s32[2]{0:T(128)} %pad_add_fusion.scal, s32[1,2048]{1,0:T(1,128)} %seg_row.5, s32[2048,1]{1,0:T(8,128)} %copy.44.seg_col, bf16[320,2048]{1,0:T(8,128)(2,1)} %get-tuple-element.80.qt_ref, ...), custom_call_target="tpu_custom_call" | custom-call | flops 17179869184 | bytes 10485760 | tf_op jit(solution)/shard_map/attend_back/pallas_call | solution.py:310
  221.4 7.7 %adapter_gradients.1 = (bf16[48,2048]{1,0:T(8,128)(2,1)}, bf16[64,1280]{1,0:T(8,128)(2,1)}) custom-call(s32[2]{0:T(128)} %pad_add_fusion.scal, bf16[320,2048]{1,0:T(8,128)(2,1)} %get-tuple-element.108.dq, bf16[320,2048]{1,0:T(8,128)(2,1)} %get-tuple-element.109.dk, bf16[320,2048]{1,0:T(8,128)(2,1)} %get-tuple-element.110.dv, ...), custom_call_target="tpu_custom_call" | custom-call | flops 1006632960 | bytes 10485760 | tf_op jit(solution)/shard_map/adapter_gradients/pallas_call | solution.py:488
  229.1 0.9 slice.18
  230.0 1.5 collective-permute-start.22
  231.5 0.4 collective-permute-start.21
  231.9 0.3 collective-permute-start.23
  232.2 7.1 %grad_input.3 = bf16[2,512,1280]{2,1,0:T(8,128)(2,1)} custom-call(s32[2]{0:T(128)} %pad_add_fusion.scal, bf16[320,2048]{1,0:T(8,128)(2,1)} %get-tuple-element.108.dq, bf16[320,2048]{1,0:T(8,128)(2,1)} %get-tuple-element.109.dk, bf16[320,2048]{1,0:T(8,128)(2,1)} %get-tuple-element.110.dv, bf16[48,2048]{1,0:T(8,128)(2,1)} %get-tuple-element.112.back, ...), custom_call_target="tpu_custom_call" | custom-call | flops 2642411520 | bytes 7864320 | tf_op jit(solution)/shard_map/grad_input/pallas_call | solution.py:522
  239.4 2.5 slice_bitcast_fusion
  241.9 0.5 collective-permute-start.16
  242.4 7.1 %grad_input.2.a_ref = bf16[2,512,1280]{2,1,0:T(8,128)(2,1)} custom-call(s32[2]{0:T(128)} %pad_add_fusion.scal, bf16[320,2048]{1,0:T(8,128)(2,1)} %get-tuple-element.108.dq, bf16[320,2048]{1,0:T(8,128)(2,1)} %get-tuple-element.109.dk, bf16[320,2048]{1,0:T(8,128)(2,1)} %get-tuple-element.110.dv, bf16[48,2048]{1,0:T(8,128)(2,1)} %get-tuple-element.112.back, ...), custom_call_target="tpu_custom_call" | custom-call | flops 2642411520 | bytes 7864320 | tf_op jit(solution)/shard_map/grad_input/pallas_call | solution.py:522
  249.6 0.1 add_convert_fusion.1
  249.7 0.7 pad_maximum_fusion
  250.4 2.6 slice_bitcast_fusion.2
  253.0 0.1 collective-permute-start.15
  253.1 2.7 fusion
  255.8 1.3 collective-permute-start.17
  257.1 6.0 %set_sums.3 = (f32[8,16,1280]{2,1,0:T(8,128)}, f32[8,16,1280]{2,1,0:T(8,128)}, f32[8,16,1280]{2,1,0:T(8,128)}, f32[8,16,320]{2,1,0:T(8,128)}, f32[8,16,320]{2,1,0:T(8,128)}, /*index=5*/f32[8,16,320]{2,1,0:T(8,128)}) custom-call(bf16[8,64,1280]{2,1,0:T(8,128)(2,1)} %bitcast.23, bf16[8,64,1280]{2,1,0:T(8,128)(2,1)} %bitcast.24), custom_call_target="tpu_custom_call" | custom-call | tf_op jit(solution)/shard_map/set_sums/pallas_call | solution.py:583
  263.1 30.5 %all-gather.10.cloned.1.call-done = bf16[512,1280]{1,0:T(8,128)(2,1)} async-done(((bf16[64,1280]{1,0:T(8,128)(2,1)}), bf16[512,1280]{1,0:T(8,128)(2,1)}) %all-gather.10.cloned.1.call-update) | async-done | bytes 1310736 | tf_op jit(solution)/shard_map/all_gather | solution.py:680
  293.6 5.9 %set_sums.2 = (f32[8,16,1280]{2,1,0:T(8,128)}, f32[8,16,1280]{2,1,0:T(8,128)}, f32[8,16,1280]{2,1,0:T(8,128)}, f32[8,16,320]{2,1,0:T(8,128)}, f32[8,16,320]{2,1,0:T(8,128)}, /*index=5*/f32[8,16,320]{2,1,0:T(8,128)}) custom-call(bf16[8,64,1280]{2,1,0:T(8,128)(2,1)} %bitcast.25, bf16[8,64,1280]{2,1,0:T(8,128)(2,1)} %bitcast.30), custom_call_target="tpu_custom_call" | custom-call | tf_op jit(solution)/shard_map/set_sums/pallas_call | solution.py:583
  299.5 1.1 copy-done.3
  300.6 5.3 %input_gradient.1 = bf16[512,1280]{1,0:T(8,128)(2,1)} custom-call(bf16[512,1280]{1,0:T(8,128)(2,1)} %bitcast.28, f32[512,1280]{1,0:T(8,128)} %get-tuple-element.99.gm_ref, bf16[2,512,1280]{2,1,0:T(8,128)(2,1)} %grad_input.2.a_ref, bf16[512,1280]{1,0:T(8,128)(2,1)} %collective-permute-done.15.b_ref, bf16[512,1280]{1,0:T(8,128)(2,1)} %copy-done.3), custom_call_target="tpu_custom_call" | custom-call | tf_op jit(solution)/shard_map/input_gradient/pallas_call | solution.py:550
  (64 shorter events, 0.3 us)
Async XLA Ops:
  7.2 97.5 %all-gather.6.cloned.1.call-start = ((), (), s32[]{:S(2)}) async-start(), calls=%async_computation | async-start | bytes 2764800 | tf_op jit(solution)/shard_map/all_gather | solution.py:640
  7.9 2.9 copy-start.4
  10.8 1.4 copy-start.5
  10.8 2.4 copy-start.6
  13.2 44.7 %copy-start.9 = (s32[1,2048]{1,0:T(1,128)S(1)}, s32[1,2048]{1,0:T(1,128)}, u32[]{:S(2)}) copy-start(s32[1,2048]{1,0:T(1,128)} %seg_row.5) | copy-start | bytes 24580
  15.2 10.3 %collective-permute-start.6 = (bf16[120,1280]{1,0:T(8,128)(2,1)S(1)}, bf16[120,1280]{1,0:T(8,128)(2,1)S(1)}, u32[]{:S(2)}, u32[]{:S(2)}) collective-permute-start(bf16[120,1280]{1,0:T(8,128)(2,1)S(1)} %constant_dynamic-slice_fusion), channel_id=1, source_target_pairs={{0,2},{1,3},{2,0},{3,1},{4,6},{5,7},{6,4},{7,5},{8,10},{9,11},{10,... | collective-permute-start | bytes 921608 | tf_op jit(solution)/shard_map/ppermute | solution.py:51
  25.5 0.7 copy-start.8
  26.2 230.9 %all-gather.8.cloned.1.call-start = ((), (), s32[]{:S(2)}) async-start(), calls=%async_computation.1 | async-start | bytes 1474560 | tf_op jit(solution)/shard_map/all_gather | solution.py:673
  26.3 31.1 %collective-permute-start = (bf16[528,1280]{1,0:T(8,128)(2,1)}, bf16[528,1280]{1,0:T(8,128)(2,1)S(1)}, u32[]{:S(2)}, u32[]{:S(2)}) collective-permute-start(bf16[528,1280]{1,0:T(8,128)(2,1)} %norm_in.1.p0.s0), channel_id=1, source_target_pairs={{0,2},{1,3},{2,0},{3,1},{4,6},{5,7},{6,4},{7,5},{8,10},{9,11},{10,... | collective-permute-start | bytes 4055048 | tf_op jit(solution)/shard_map/ppermute | solution.py:51
  28.1 31.8 %collective-permute-start.2 = (bf16[528,1280]{1,0:T(8,128)(2,1)}, bf16[528,1280]{1,0:T(8,128)(2,1)}, u32[]{:S(2)}, u32[]{:S(2)}) collective-permute-start(bf16[528,1280]{1,0:T(8,128)(2,1)} %norm_in.1.p0.s0), channel_id=1, source_target_pairs={{0,1},{1,0},{2,3},{3,2},{4,5},{5,4},{6,7},{7,6},{8,9},{9,8},{10,11... | collective-permute-start | bytes 4055048 | tf_op jit(solution)/shard_map/ppermute | solution.py:51
  57.4 12.7 %copy-start = (bf16[528,1280]{1,0:T(8,128)(2,1)}, bf16[528,1280]{1,0:T(8,128)(2,1)S(1)}, u32[]{:S(2)}) copy-start(bf16[528,1280]{1,0:T(8,128)(2,1)S(1)} %collective-permute-done.p0.s2.p2) | copy-start | bytes 4055044
  57.4 12.7 %collective-permute-start.1 = (bf16[528,1280]{1,0:T(8,128)(2,1)S(1)}, bf16[528,1280]{1,0:T(8,128)(2,1)S(1)}, u32[]{:S(2)}, u32[]{:S(2)}) collective-permute-start(bf16[528,1280]{1,0:T(8,128)(2,1)S(1)} %collective-permute-done.p0.s2.p2), channel_id=1, source_target_pairs={{0,1},{1,0},{2,3},{3,2},{4,5},{5,4},{6,7},{7,6},{8,9},{9,8},{10,11... | collective-permute-start | bytes 4055048 | tf_op jit(solution)/shard_map/ppermute | solution.py:51
  57.4 49.4 %collective-permute-start.10 = (bf16[960,1280]{1,0:T(8,128)(2,1)}, bf16[960,1280]{1,0:T(8,128)(2,1)}, u32[]{:S(2)}, u32[]{:S(2)}) collective-permute-start(bf16[960,1280]{1,0:T(8,128)(2,1)} %constant_dynamic-update-slice_fusion.w0), channel_id=1, source_target_pairs={{0,1},{1,0},{2,3},{3,2},{4,5},{5,4},{6,7},{7,6},{8,9},{9,8},{10,11... | collective-permute-start | bytes 7372808 | tf_op jit(solution)/shard_map/ppermute | solution.py:51
  70.1 1.2 copy-start.1
  92.4 12.4 %copy-start.21 = (bf16[512,160]{1,0:T(8,128)(2,1)S(1)}, bf16[512,160]{1,0:T(8,128)(2,1)}, u32[]{:S(2)}) copy-start(bf16[512,160]{1,0:T(8,128)(2,1)} %get-tuple-element.84) | copy-start | bytes 491524
  92.4 14.3 %copy-start.18 = (bf16[512,160]{1,0:T(8,128)(2,1)S(1)}, bf16[512,160]{1,0:T(8,128)(2,1)}, u32[]{:S(2)}) copy-start(bf16[512,160]{1,0:T(8,128)(2,1)} %get-tuple-element.86) | copy-start | bytes 491524
  104.7 25.1 %collective-permute-start.11 = (bf16[960,1280]{1,0:T(8,128)(2,1)}, bf16[960,1280]{1,0:T(8,128)(2,1)S(1)}, u32[]{:S(2)}, u32[]{:S(2)}) collective-permute-start(bf16[960,1280]{1,0:T(8,128)(2,1)} %all-gather.6.cloned.1.call-done.w2), channel_id=1, source_target_pairs={{0,1},{1,0},{2,3},{3,2},{4,5},{5,4},{6,7},{7,6},{8,9},{9,8},{10,11... | collective-permute-start | bytes 7372808 | tf_op jit(solution)/shard_map/ppermute | solution.py:51
  104.8 5.0 %collective-permute-start.3 = (bf16[512,160]{1,0:T(8,128)(2,1)S(1)}, bf16[512,160]{1,0:T(8,128)(2,1)S(1)}, u32[]{:S(2)}, u32[]{:S(2)}) collective-permute-start(bf16[512,160]{1,0:T(8,128)(2,1)S(1)} %copy-done.21), channel_id=1, source_target_pairs={{0,1},{1,0},{2,3},{3,2},{4,5},{5,4},{6,7},{7,6},{8,9},{9,8},{10,11... | collective-permute-start | bytes 491528 | tf_op jit(solution)/shard_map/ppermute | solution.py:51
  105.3 9.4 %collective-permute-start.4 = (bf16[512,160]{1,0:T(8,128)(2,1)}, bf16[512,160]{1,0:T(8,128)(2,1)S(1)}, u32[]{:S(2)}, u32[]{:S(2)}) collective-permute-start(bf16[512,160]{1,0:T(8,128)(2,1)} %get-tuple-element.85), channel_id=1, source_target_pairs={{0,2},{1,3},{2,0},{3,1},{4,6},{5,7},{6,4},{7,5},{8,10},{9,11},{10,... | collective-permute-start | bytes 491528 | tf_op jit(solution)/shard_map/ppermute | solution.py:51
  106.7 12.5 %collective-permute-start.5 = (bf16[512,160]{1,0:T(8,128)(2,1)S(1)}, bf16[512,160]{1,0:T(8,128)(2,1)S(1)}, u32[]{:S(2)}, u32[]{:S(2)}) collective-permute-start(bf16[512,160]{1,0:T(8,128)(2,1)S(1)} %copy-done.18), channel_id=1, source_target_pairs={{0,3},{1,2},{2,1},{3,0},{4,7},{5,6},{6,5},{7,4},{8,11},{9,10},{10,... | collective-permute-start | bytes 491528 | tf_op jit(solution)/shard_map/ppermute | solution.py:51
  106.7 12.5 %collective-permute-start.7 = (bf16[512,160]{1,0:T(8,128)(2,1)}, bf16[512,160]{1,0:T(8,128)(2,1)S(1)}, u32[]{:S(2)}, u32[]{:S(2)}) collective-permute-start(bf16[512,160]{1,0:T(8,128)(2,1)} %get-tuple-element.94), channel_id=1, source_target_pairs={{0,1},{1,0},{2,3},{3,2},{4,5},{5,4},{6,7},{7,6},{8,9},{9,8},{10,11... | collective-permute-start | bytes 491528 | tf_op jit(solution)/shard_map/ppermute | solution.py:51
  109.8 20.6 %copy-start.14 = (bf16[512,160]{1,0:T(8,128)(2,1)}, bf16[512,160]{1,0:T(8,128)(2,1)S(1)}, u32[]{:S(2)}) copy-start(bf16[512,160]{1,0:T(8,128)(2,1)S(1)} %collective-permute-done.3.a1) | copy-start | bytes 491524
  109.8 16.1 %collective-permute-start.8 = (bf16[512,160]{1,0:T(8,128)(2,1)}, bf16[512,160]{1,0:T(8,128)(2,1)S(1)}, u32[]{:S(2)}, u32[]{:S(2)}) collective-permute-start(bf16[512,160]{1,0:T(8,128)(2,1)} %get-tuple-element.95), channel_id=1, source_target_pairs={{0,2},{1,3},{2,0},{3,1},{4,6},{5,7},{6,4},{7,5},{8,10},{9,11},{10,... | collective-permute-start | bytes 491528 | tf_op jit(solution)/shard_map/ppermute | solution.py:51
  114.7 15.8 %copy-start.15 = (bf16[512,160]{1,0:T(8,128)(2,1)}, bf16[512,160]{1,0:T(8,128)(2,1)S(1)}, u32[]{:S(2)}) copy-start(bf16[512,160]{1,0:T(8,128)(2,1)S(1)} %collective-permute-done.4.a2) | copy-start | bytes 491524
  114.7 15.1 %collective-permute-start.9 = (bf16[512,160]{1,0:T(8,128)(2,1)}, bf16[512,160]{1,0:T(8,128)(2,1)S(1)}, u32[]{:S(2)}, u32[]{:S(2)}) collective-permute-start(bf16[512,160]{1,0:T(8,128)(2,1)} %get-tuple-element.96), channel_id=1, source_target_pairs={{0,3},{1,2},{2,1},{3,0},{4,7},{5,6},{6,5},{7,4},{8,11},{9,10},{10,... | collective-permute-start | bytes 491528 | tf_op jit(solution)/shard_map/ppermute | solution.py:51
  119.2 11.3 %copy-start.16 = (bf16[512,160]{1,0:T(8,128)(2,1)}, bf16[512,160]{1,0:T(8,128)(2,1)S(1)}, u32[]{:S(2)}) copy-start(bf16[512,160]{1,0:T(8,128)(2,1)S(1)} %collective-permute-done.5.a3) | copy-start | bytes 491524
  119.2 11.3 %copy-start.17 = (bf16[512,160]{1,0:T(8,128)(2,1)}, bf16[512,160]{1,0:T(8,128)(2,1)S(1)}, u32[]{:S(2)}) copy-start(bf16[512,160]{1,0:T(8,128)(2,1)S(1)} %collective-permute-done.7.b1) | copy-start | bytes 491524
  125.9 4.6 %copy-start.19 = (bf16[512,160]{1,0:T(8,128)(2,1)}, bf16[512,160]{1,0:T(8,128)(2,1)S(1)}, u32[]{:S(2)}) copy-start(bf16[512,160]{1,0:T(8,128)(2,1)S(1)} %collective-permute-done.8.b2) | copy-start | bytes 491524
  129.8 0.7 copy-start.20
  130.5 1.6 copy-start.10
  165.0 4.3 %collective-permute-start.18 = (bf16[64,1280]{1,0:T(8,128)(2,1)}, bf16[64,1280]{1,0:T(8,128)(2,1)S(1)}, u32[]{:S(2)}, u32[]{:S(2)}) collective-permute-start(bf16[64,1280]{1,0:T(8,128)(2,1)} %get-tuple-element.114), channel_id=1, source_target_pairs={{0,1},{1,0},{2,3},{3,2},{4,5},{5,4},{6,7},{7,6},{8,9},{9,8},{10,11... | collective-permute-start | bytes 491528 | tf_op jit(solution)/shard_map/ppermute | solution.py:51
  165.8 7.3 %collective-permute-start.19 = (bf16[64,1280]{1,0:T(8,128)(2,1)}, bf16[64,1280]{1,0:T(8,128)(2,1)S(1)}, u32[]{:S(2)}, u32[]{:S(2)}) collective-permute-start(bf16[64,1280]{1,0:T(8,128)(2,1)} %get-tuple-element.115), channel_id=1, source_target_pairs={{0,2},{1,3},{2,0},{3,1},{4,6},{5,7},{6,4},{7,5},{8,10},{9,11},{10,... | collective-permute-start | bytes 491528 | tf_op jit(solution)/shard_map/ppermute | solution.py:51
  167.2 8.4 %collective-permute-start.20 = (bf16[64,1280]{1,0:T(8,128)(2,1)}, bf16[64,1280]{1,0:T(8,128)(2,1)S(1)}, u32[]{:S(2)}, u32[]{:S(2)}) collective-permute-start(bf16[64,1280]{1,0:T(8,128)(2,1)} %get-tuple-element.116), channel_id=1, source_target_pairs={{0,3},{1,2},{2,1},{3,0},{4,7},{5,6},{6,5},{7,4},{8,11},{9,10},{10,... | collective-permute-start | bytes 491528 | tf_op jit(solution)/shard_map/ppermute | solution.py:51
  167.2 10.1 %collective-permute-start.12 = (bf16[512,320]{1,0:T(8,128)(2,1)}, bf16[512,320]{1,0:T(8,128)(2,1)S(1)}, u32[]{:S(2)}, u32[]{:S(2)}) collective-permute-start(bf16[512,320]{1,0:T(8,128)(2,1)} %get-tuple-element.105), channel_id=1, source_target_pairs={{0,1},{1,0},{2,3},{3,2},{4,5},{5,4},{6,7},{7,6},{8,9},{9,8},{10,11... | collective-permute-start | bytes 983048 | tf_op jit(solution)/shard_map/ppermute | solution.py:51
  167.9 17.1 %collective-permute-start.13 = (bf16[512,320]{1,0:T(8,128)(2,1)}, bf16[512,320]{1,0:T(8,128)(2,1)S(1)}, u32[]{:S(2)}, u32[]{:S(2)}) collective-permute-start(bf16[512,320]{1,0:T(8,128)(2,1)} %get-tuple-element.106), channel_id=1, source_target_pairs={{0,2},{1,3},{2,0},{3,1},{4,6},{5,7},{6,4},{7,5},{8,10},{9,11},{10,... | collective-permute-start | bytes 983048 | tf_op jit(solution)/shard_map/ppermute | solution.py:51
  169.3 22.3 %collective-permute-start.14 = (bf16[512,320]{1,0:T(8,128)(2,1)}, bf16[512,320]{1,0:T(8,128)(2,1)S(1)}, u32[]{:S(2)}, u32[]{:S(2)}) collective-permute-start(bf16[512,320]{1,0:T(8,128)(2,1)} %get-tuple-element.107), channel_id=1, source_target_pairs={{0,3},{1,2},{2,1},{3,0},{4,7},{5,6},{6,5},{7,4},{8,11},{9,10},{10,... | collective-permute-start | bytes 983048 | tf_op jit(solution)/shard_map/ppermute | solution.py:51
  177.3 116.3 %all-gather.10.cloned.1.call-start = ((), (), s32[]{:S(2)}) async-start(), calls=%async_computation.2 | async-start | bytes 1474560 | tf_op jit(solution)/shard_map/all_gather | solution.py:680
  177.4 14.3 %copy-start.11 = (bf16[512,320]{1,0:T(8,128)(2,1)}, bf16[512,320]{1,0:T(8,128)(2,1)S(1)}, u32[]{:S(2)}) copy-start(bf16[512,320]{1,0:T(8,128)(2,1)S(1)} %collective-permute-done.12.d1) | copy-start | bytes 983044
  185.0 6.7 %copy-start.12 = (bf16[512,320]{1,0:T(8,128)(2,1)}, bf16[512,320]{1,0:T(8,128)(2,1)S(1)}, u32[]{:S(2)}) copy-start(bf16[512,320]{1,0:T(8,128)(2,1)S(1)} %collective-permute-done.13.d2) | copy-start | bytes 983044
  191.7 0.7 copy-start.13
  230.0 19.5 %collective-permute-start.22 = (bf16[48,1280]{1,0:T(8,128)(2,1)S(1)}, bf16[48,1280]{1,0:T(8,128)(2,1)S(1)}, u32[]{:S(2)}, u32[]{:S(2)}) collective-permute-start(bf16[48,1280]{1,0:T(8,128)(2,1)S(1)} %slice.18), channel_id=1, source_target_pairs={{0,2},{1,3},{2,0},{3,1},{4,6},{5,7},{6,4},{7,5},{8,10},{9,11},{10,... | collective-permute-start | bytes 368648 | tf_op jit(solution)/shard_map/ppermute | solution.py:51
  231.5 18.0 %collective-permute-start.21 = (bf16[48,1280]{1,0:T(8,128)(2,1)S(1)}, bf16[48,1280]{1,0:T(8,128)(2,1)S(1)}, u32[]{:S(2)}, u32[]{:S(2)}) collective-permute-start(bf16[48,1280]{1,0:T(8,128)(2,1)S(1)} %slice.18), channel_id=1, source_target_pairs={{0,1},{1,0},{2,3},{3,2},{4,5},{5,4},{6,7},{7,6},{8,9},{9,8},{10,11... | collective-permute-start | bytes 368648 | tf_op jit(solution)/shard_map/ppermute | solution.py:51
  231.9 17.7 %collective-permute-start.23 = (bf16[48,1280]{1,0:T(8,128)(2,1)S(1)}, bf16[48,1280]{1,0:T(8,128)(2,1)S(1)}, u32[]{:S(2)}, u32[]{:S(2)}) collective-permute-start(bf16[48,1280]{1,0:T(8,128)(2,1)S(1)} %slice.18), channel_id=1, source_target_pairs={{0,3},{1,2},{2,1},{3,0},{4,7},{5,6},{6,5},{7,4},{8,11},{9,10},{10,... | collective-permute-start | bytes 368648 | tf_op jit(solution)/shard_map/ppermute | solution.py:51
  241.9 7.7 %copy-start.7 = (bf16[64,1280]{1,0:T(8,128)(2,1)S(1)}, bf16[64,1280]{1,0:T(8,128)(2,1)}, u32[]{:S(2)}) copy-start(bf16[64,1280]{1,0:T(8,128)(2,1)} %get-tuple-element.117) | copy-start | bytes 491524
  241.9 11.2 %collective-permute-start.16 = (bf16[512,1280]{1,0:T(8,128)(2,1)}, bf16[512,1280]{1,0:T(8,128)(2,1)}, u32[]{:S(2)}, u32[]{:S(2)}) collective-permute-start(bf16[512,1280]{1,0:T(8,128)(2,1)} %slice_bitcast_fusion), channel_id=1, source_target_pairs={{0,1},{1,0},{2,3},{3,2},{4,5},{5,4},{6,7},{7,6},{8,9},{9,8},{10,11... | collective-permute-start | bytes 3932168 | tf_op jit(solution)/shard_map/ppermute | solution.py:51
  250.3 2.8 copy-start.2
  253.0 46.5 %collective-permute-start.15 = (bf16[512,1280]{1,0:T(8,128)(2,1)}, bf16[512,1280]{1,0:T(8,128)(2,1)}, u32[]{:S(2)}, u32[]{:S(2)}) collective-permute-start(bf16[512,1280]{1,0:T(8,128)(2,1)} %slice_bitcast_fusion.2), channel_id=1, source_target_pairs={{0,1},{1,0},{2,3},{3,2},{4,5},{5,4},{6,7},{7,6},{8,9},{9,8},{10,11... | collective-permute-start | bytes 3932168 | tf_op jit(solution)/shard_map/ppermute | solution.py:51
  255.8 43.7 %collective-permute-start.17 = (bf16[512,1280]{1,0:T(8,128)(2,1)}, bf16[512,1280]{1,0:T(8,128)(2,1)S(1)}, u32[]{:S(2)}, u32[]{:S(2)}) collective-permute-start(bf16[512,1280]{1,0:T(8,128)(2,1)} %fusion), channel_id=1, source_target_pairs={{0,2},{1,3},{2,0},{3,1},{4,6},{5,7},{6,4},{7,5},{8,10},{9,11},{10,... | collective-permute-start | bytes 3932168 | tf_op jit(solution)/shard_map/ppermute | solution.py:51
  299.5 1.1 copy-start.3
Sparse Core Ops, SparseCore 0:
  26.3 54.5 all-gather.5
  177.4 43.6 all-gather.7
  250.5 43.0 all-gather.9
